TPU v7x, 32 devices: a whole 2x2x4 slice. The times are simulated.
32 devices in a mesh: cells: 8 (over z, x), slots: 4 (over y, core).
Axes of the slice: x: 2, y: 2, z: 4, core: 2. Of those that a mesh axis runs over, the one named last changes fastest.
Arguments:
- tokens: bfloat16 [16, 2048, 256], P('cells', 'slots'), may hold values from -6 to 6
- valid_len: int32 [16], P('cells'), may hold values from 256 to 2048, as said below
- library: int32 [16], P('cells'), may hold values from 512 to 33279
- gene_slot: int32 [16, 2048], P('cells'), may hold values from 0 to 2047, as said below
- counts: int32 [16, 2048], P('cells', 'slots'), may hold values from 0 to 71, as said below
- norm1_gain: float32 [256], replicated, may hold values from 0.5 to 1.5
- w_qkv: bfloat16 [256, 768], replicated, may hold values from -0.375 to 0.375
- w_out: bfloat16 [256, 256], replicated, may hold values from -1.5 to 1.5
- norm2_gain: float32 [256], replicated, may hold values from 0.5 to 1.5
- w_up: bfloat16 [256, 1024], replicated, may hold values from -0.375 to 0.375
- w_down: bfloat16 [1024, 256], replicated, may hold values from -0.1875 to 0.1875
- w_decoder: bfloat16 [3, 256], replicated, may hold values from -0.375 to 0.375
Outputs:
- grad_tokens: float32 [16, 2048, 256], P('cells', 'slots')
- grad_norm1_gain: float32 [256], replicated
- grad_w_qkv: float32 [256, 768], replicated
- grad_w_out: float32 [256, 256], replicated
- grad_norm2_gain: float32 [256], replicated
- grad_w_up: float32 [256, 1024], replicated
- grad_w_down: float32 [1024, 256], replicated
- grad_w_decoder: float32 [3, 256], replicated
- summary: float32 [4], replicated
Inputs may be any that keep to these rules, and one draw needn't show every extreme that they name: `valid_len`: in each aligned block of 2 cells one cell has all 2048 slots valid. `gene_slot`: each row is a permutation of the gene numbers 0 to 2047; the 512 slots of an aligned block hold exactly 128 gene numbers of each aligned block of 512 gene numbers. `counts`: indexed by cell and gene number.
All inputs are finite; a program needn't handle non-finite values.
Results may differ from a plain program's by a relative error of at most 0.0055.
Values may be sent and summed in bfloat16 or wider, within the bound.
No kernel may reach another device: no remote copies, remote signals or barrier semaphores. Data moves between devices by JAX's collectives and lax.ppermute only.
A program may use at most 128 MiB of HBM per device.

v0:
```python
import jax
import jax.numpy as jnp
from jax import lax
from jax.sharding import PartitionSpec as P

HEADS = 4


EPS = 1e-05
HIGH_PRECISION = lax.Precision.HIGHEST


def layer_norm(hidden, gain):
    centre = jnp.mean(hidden, axis=-1, keepdims=True)
    centred = hidden - centre
    spread = jnp.mean(centred * centred, axis=-1, keepdims=True)
    return centred * lax.rsqrt(spread + EPS) * gain


def zinb_nll(decoder_output, observed, scale):
    mean_raw = decoder_output[..., 0]
    disp_raw = decoder_output[..., 1]
    drop_raw = decoder_output[..., 2]
    rate = scale * (jax.nn.softplus(mean_raw) + 0.05)
    theta = jax.nn.softplus(disp_raw) + 0.05
    log_total = jnp.log(theta + rate)
    log_zero_nb = theta * (jnp.log(theta) - log_total)
    dropout = jax.nn.sigmoid(drop_raw)
    zero_case = -jnp.log(dropout + (1.0 - dropout) * jnp.exp(log_zero_nb))
    observed_f = observed.astype(jnp.float32)
    log_nb = (
        lax.lgamma(observed_f + theta)
        - lax.lgamma(theta)
        - lax.lgamma(observed_f + 1.0)
        + log_zero_nb
        + observed_f * (jnp.log(rate) - log_total)
    )
    nonzero_case = jax.nn.softplus(drop_raw) - log_nb
    return jnp.where(observed > 0, nonzero_case, zero_case)


def decoder_total(decoder_input, weight_params, observed, scale, valid):
    decoder_output = jnp.einsum(
        "awm,em->awe", decoder_input, weight_params, precision=HIGH_PRECISION
    )
    return jnp.sum(valid * zinb_nll(decoder_output, observed, scale))


def per_device(
    tokens,
    valid_len,
    library,
    gene_slot,
    counts,
    norm1_gain,
    w_qkv,
    w_out,
    norm2_gain,
    w_up,
    w_down,
    w_decoder,
):
    cells, local_length, width = tokens.shape
    slot_count = lax.axis_size("slots")
    slot_index = lax.axis_index("slots")
    length = local_length * slot_count
    share = local_length // slot_count
    head_dim = width // HEADS
    factor = head_dim ** (-0.5)
    positions = slot_index * local_length + jnp.arange(local_length, dtype=jnp.int32)
    valid = (positions[None, :] < valid_len[:, None]).astype(jnp.float32)
    scale = library.astype(jnp.float32) / length
    source = tokens.astype(jnp.float32)
    normed = layer_norm(source, norm1_gain).astype(jnp.bfloat16)
    mixed = jnp.dot(normed, w_qkv, preferred_element_type=jnp.float32).astype(jnp.bfloat16)
    query = mixed[..., :width].reshape(cells, local_length, HEADS, head_dim)
    key_value = mixed[..., width:]

    def live_mask(span):
        places = jnp.arange(span, dtype=jnp.int32)
        return (places[None, :] < valid_len[:, None])[:, None, None, :]

    piece = lax.all_gather(key_value, "slots", axis=1, tiled=True)
    best = jnp.full((cells, HEADS, local_length), -1e30, jnp.float32)
    span = piece.shape[1]
    key_rows = piece[..., :width].reshape(cells, span, HEADS, head_dim)
    value_rows = piece[..., width:].reshape(cells, span, HEADS, head_dim).astype(jnp.float32)
    live = live_mask(span)
    scores = (
        jnp.einsum("cqhd,ckhd->chqk", query, key_rows, preferred_element_type=jnp.float32) * factor
    )
    scores = jnp.where(live, scores, -1e30)
    newest = jnp.maximum(best, jnp.max(scores, axis=-1))
    attention = jnp.where(live, jnp.exp(scores - newest[..., None]), 0.0)
    total = jnp.sum(attention, axis=-1)
    summed = jnp.einsum("chqk,ckhd->chqd", attention, value_rows, precision=HIGH_PRECISION)
    best, total, summed = (newest, total, summed)
    log_sum = best + jnp.log(total)
    heads_out = summed / total[..., None]
    attended = (
        jnp.transpose(heads_out, (0, 2, 1, 3))
        .reshape(cells, local_length, width)
        .astype(jnp.bfloat16)
    )
    attn_out = jnp.dot(attended, w_out, preferred_element_type=jnp.float32)
    resid = source + attn_out
    normed_two = layer_norm(resid, norm2_gain).astype(jnp.bfloat16)
    up = jnp.dot(normed_two, w_up, preferred_element_type=jnp.float32)
    act = jax.nn.gelu(up, approximate=False).astype(jnp.bfloat16)
    mlp_out = jnp.dot(act, w_down, preferred_element_type=jnp.float32)
    final = resid + mlp_out
    decoder_low = final.astype(jnp.bfloat16)
    grouped = gene_slot.reshape(cells, slot_count, local_length)
    places_sorted = jnp.argsort(grouped, axis=-1)
    genes_sorted = jnp.take_along_axis(grouped, places_sorted, axis=-1)
    own_order = lax.dynamic_index_in_dim(places_sorted, slot_index, 1, keepdims=False)
    own_inverse = jnp.argsort(own_order, axis=1)
    arrived_genes = lax.dynamic_slice_in_dim(genes_sorted, slot_index * share, share, 2).reshape(
        cells, local_length
    )
    arrived_places = (
        lax.dynamic_slice_in_dim(places_sorted, slot_index * share, share, 2)
        + (jnp.arange(slot_count, dtype=jnp.int32) * local_length)[None, :, None]
    ).reshape(cells, local_length)
    arrived_counts = jnp.take_along_axis(counts, arrived_genes - slot_index * local_length, axis=1)
    decoder_weights = w_decoder.astype(jnp.float32)
    sorted_low = jnp.take_along_axis(decoder_low, own_order[..., None], axis=1)
    arrived = lax.all_to_all(sorted_low, "slots", split_axis=1, concat_axis=1, tiled=True)
    arrived_valid = (arrived_places < valid_len[:, None]).astype(jnp.float32)
    nll_total, decoder_pull = jax.vjp(
        lambda rows, weight_params: decoder_total(
            rows, weight_params, arrived_counts, scale[:, None], arrived_valid
        ),
        arrived.astype(jnp.float32),
        decoder_weights,
    )
    grad_rows, grad_w_decoder = decoder_pull(jnp.ones_like(nll_total))
    returned = lax.all_to_all(
        grad_rows.astype(jnp.bfloat16), "slots", split_axis=1, concat_axis=1, tiled=True
    )
    grad_decoder_in = jnp.take_along_axis(returned, own_inverse[..., None], axis=1)
    grad_final = grad_decoder_in.astype(jnp.float32)
    grad_w_down = jnp.einsum(
        "clf,cld->fd", act, grad_decoder_in, preferred_element_type=jnp.float32
    )
    grad_act = jnp.einsum(
        "cld,fd->clf", grad_decoder_in, w_down, preferred_element_type=jnp.float32
    )
    _, gelu_pull = jax.vjp(lambda inner: jax.nn.gelu(inner, approximate=False), up)
    grad_up = gelu_pull(grad_act)[0].astype(jnp.bfloat16)
    grad_w_up = jnp.einsum("cld,clf->df", normed_two, grad_up, preferred_element_type=jnp.float32)
    grad_normed_two = jnp.einsum("clf,df->cld", grad_up, w_up, preferred_element_type=jnp.float32)
    _, norm_two_pull = jax.vjp(layer_norm, resid, norm2_gain)
    grad_resid_norm, grad_gain_two = norm_two_pull(grad_normed_two)
    grad_resid = grad_final + grad_resid_norm
    grad_attn_low = grad_resid.astype(jnp.bfloat16)
    grad_w_out = jnp.einsum(
        "cld,cle->de", attended, grad_attn_low, preferred_element_type=jnp.float32
    )
    grad_attended = jnp.einsum(
        "cle,de->cld", grad_attn_low, w_out, preferred_element_type=jnp.float32
    ).astype(jnp.bfloat16)
    grad_heads = grad_attended.reshape(cells, local_length, HEADS, head_dim)
    grad_heads_f = grad_heads.astype(jnp.float32)
    delta = jnp.einsum("cqhd,chqd->chq", grad_heads_f, heads_out, precision=HIGH_PRECISION)
    piece = lax.all_gather(key_value, "slots", axis=1, tiled=True)
    span = piece.shape[1]
    key_rows = piece[..., :width].reshape(cells, span, HEADS, head_dim)
    value_rows = piece[..., width:].reshape(cells, span, HEADS, head_dim)
    live = live_mask(span)
    scores = (
        jnp.einsum("cqhd,ckhd->chqk", query, key_rows, preferred_element_type=jnp.float32) * factor
    )
    attention = jnp.where(live, jnp.exp(scores - log_sum[..., None]), 0.0)
    grad_attention = jnp.einsum(
        "cqhd,ckhd->chqk", grad_heads, value_rows, preferred_element_type=jnp.float32
    )
    grad_scores = (attention * (grad_attention - delta[..., None])).astype(jnp.bfloat16)
    grad_query = (
        jnp.einsum("chqk,ckhd->cqhd", grad_scores, key_rows, preferred_element_type=jnp.float32)
        * factor
    )
    grad_key = (
        jnp.einsum("chqk,cqhd->ckhd", grad_scores, query, preferred_element_type=jnp.float32)
        * factor
    )
    grad_value = jnp.einsum("chqk,cqhd->ckhd", attention, grad_heads_f, precision=HIGH_PRECISION)
    block = jnp.concatenate(
        [grad_key.reshape(cells, span, width), grad_value.reshape(cells, span, width)], axis=-1
    )
    grad_query, grad_kv_all = (grad_query, block)
    grad_kv_own = lax.psum_scatter(grad_kv_all, "slots", scatter_dimension=1, tiled=True)
    grad_mixed = jnp.concatenate(
        [grad_query.reshape(cells, local_length, width), grad_kv_own], axis=-1
    ).astype(jnp.bfloat16)
    grad_w_qkv = jnp.einsum("cld,cle->de", normed, grad_mixed, preferred_element_type=jnp.float32)
    grad_normed = jnp.einsum("cle,de->cld", grad_mixed, w_qkv, preferred_element_type=jnp.float32)
    _, norm_one_pull = jax.vjp(layer_norm, source, norm1_gain)
    grad_source_norm, grad_gain_one = norm_one_pull(grad_normed)
    grad_tokens = grad_resid + grad_source_norm
    stats = jnp.stack(
        [
            nll_total,
            jnp.sum(valid),
            jnp.sum(valid[..., None] * final * final),
            jnp.sum(valid[..., None] * attn_out * attn_out),
            jnp.sum(valid[..., None] * mlp_out * mlp_out),
        ]
    )
    sums = lax.psum(
        (
            grad_w_qkv,
            grad_w_out,
            grad_w_up,
            grad_w_down,
            grad_w_decoder,
            grad_gain_one,
            grad_gain_two,
            stats,
        ),
        ("cells", "slots"),
    )
    totals = sums[7]
    summary = jnp.stack(
        [
            totals[0] / totals[1],
            jnp.sqrt(totals[2] / (totals[1] * width)),
            jnp.sqrt(totals[3] / (totals[1] * width)),
            jnp.sqrt(totals[4] / (totals[1] * width)),
        ]
    )
    return (grad_tokens, sums[5], sums[0], sums[1], sums[6], sums[2], sums[3], sums[4], summary)


def solution(mesh):
    in_specs = (
        P("cells", "slots", None),
        P("cells"),
        P("cells"),
        P("cells", None),
        P("cells", "slots"),
        P(),
        P(),
        P(),
        P(),
        P(),
        P(),
        P(),
    )
    out_specs = (P("cells", "slots", None), P(), P(), P(), P(), P(), P(), P(), P())
    return jax.shard_map(
        per_device, mesh=mesh, in_specs=in_specs, out_specs=out_specs, check_vma=False
    )
```

profile of v0, /device:TPU:0, one launch (start us, length us, event | category | flops | bytes accessed | tf_op | source)
XLA Modules:
  0.0 518.8 jit_solution(3670211415601867126)
XLA Ops:
  21.1 40.3 %gather_fusion = s32[4096]{0:T(1024)S(1)} fusion(s32[2,4,512]{2,1,0:T(4,128)S(1)} %copy-done.2, s32[4096]{0:T(1024)S(1)} %bitcast.229), kind=kCustom, calls=%fused_computation.2 | custom fusion | bytes 81920 | tf_op jit(solution)/shard_map/jit(take_along_axis)/gather | solution.py:115
  62.3 4.5 fusion.132
  66.8 2.9 copy.142
  69.7 4.6 copy.143
  74.3 14.3 %select_reduce_fusion = (f32[2,4,512]{2,1,0:T(4,128)S(1)}, f32[2,4,512,2048]{3,2,1,0:T(8,128)}) fusion(pred[2,2048]{1,0:T(4,128)(4,1)S(1)} %iota_compare_fusion, bf16[2,512,4,64]{1,3,2,0:T(8,128)(2,1)} %bitcast.236, bf16[2,2048,4,64]{1,3,2,0:T(8,128)(2,1)S(1)} %bitcast.233), kind=kOutput, calls=%fused_computation.7 | convolution fusion | flops 1098903552 | bytes 36196352 | tf_op jit(solution)/shard_map/cqhd,ckhd->chqk/dot_general | solution.py:90
  88.7 15.0 %fusion.1 = f32[2,4,512]{2,1,0:T(4,128)S(1)} fusion(f32[2,4,512,2048]{3,2,1,0:T(8,128)} %get-tuple-element.115, f32[2,4,512]{2,1,0:T(4,128)S(1)} %broadcast_maximum_fusion, pred[2,2048]{1,0:T(4,128)(4,1)S(1)} %iota_compare_fusion), kind=kLoop, calls=%fused_computation.9 | loop fusion | flops 41938944 | bytes 33591296 | tf_op jit(solution)/shard_map/reduce_sum | solution.py:95
  103.6 33.3 %fusion.33 = (bf16[2,512,4,64]{1,3,2,0:T(8,128)(2,1)S(1)}, f32[2,4,512,64]{2,3,1,0:T(8,128)}) fusion(f32[2,512,4]{1,2,0:T(4,128)S(1)} %bitcast.248, bf16[2,2048,4,64]{1,3,2,0:T(8,128)(2,1)} %bitcast.244, f32[2,4,512,2048]{3,2,1,0:T(8,128)} %get-tuple-element.115, f32[2,4,512]{2,1,0:T(4,128)S(1)} %broadcast_maximum_fusion, ...), kind=kOutput, calls=%fused_computation.78 | convolution fusion | flops 6476529664 | bytes 37261312 | tf_op jit(solution)/shard_map/chqk,ckhd->chqd/dot_general | solution.py:96
  140.4 10.5 %multiply_convert_fusion.1 = (bf16[2,512,1024]{2,1,0:T(8,128)(2,1)S(1)}, f32[2,512,1024]{2,1,0:T(8,128)}) fusion(f32[2,512,1024]{2,1,0:T(8,128)S(1)} %get-tuple-element.119, u8[512,1024]{1,0:T(8,128)(4,1)S(1)} %get-tuple-element.72, u8[512,1024]{1,0:T(8,128)(4,1)S(1)} %get-tuple-element.71), kind=kLoop, calls=%fused_computation.29 | loop fusion | flops 73400320 | bytes 11534336 | tf_op jit(solution)/shard_map/convert_element_type | solution.py:109
  154.1 10.7 %gather_fusion.2 = bf16[1024,256]{1,0:T(8,128)(2,1)} fusion(bf16[2,512,256]{2,1,0:T(8,128)(2,1)S(1)} %copy.148, s32[1024]{0:T(1024)S(1)} %bitcast.230), kind=kCustom, calls=%fused_computation.clone | custom fusion | bytes 1056768 | tf_op jit(solution)/shard_map/jit(take_along_axis)/gather | solution.py:127
  164.8 5.4 %broadcast_select_fusion = bf16[2,512,256]{2,0,1:T(2,128)(2,1)} fusion(pred[2,512]{0,1:T(8,128)(4,1)S(1)} %copy.138, bf16[2,512,256]{2,1,0:T(8,128)(2,1)} %bitcast.241), kind=kLoop, calls=%fused_computation.87 | loop fusion | flops 262144 | bytes 1049600 | tf_op jit(solution)/shard_map/jit(take_along_axis)/select_n | solution.py:127
  170.2 4.2 all-to-all-start
  174.5 9.1 %gather_fusion.1 = s32[1024]{0:T(1024)S(1)} fusion(s32[2,512]{1,0:T(2,128)S(1)} %copy-done.3, s32[1024]{0:T(1024)S(1)} %bitcast.232), kind=kCustom, calls=%fused_computation.3 | custom fusion | bytes 16384 | tf_op jit(solution)/shard_map/jit(take_along_axis)/gather | solution.py:125
  187.9 4.1 all-to-all-start.1
  192.8 8.1 %all-to-all-done.1 = bf16[2,512,256]{2,0,1:T(2,128)(2,1)} async-done(((bf16[2,512,256]{2,0,1:T(2,128)(2,1)}), bf16[2,512,256]{2,0,1:T(2,128)(2,1)}, u32[]{:S(2)}, u32[]{:S(2)}) %all-to-all-start.1) | async-done | bytes 524320 | tf_op jit(solution)/shard_map/all_to_all | solution.py:138
  202.1 11.0 %gather_fusion.3 = bf16[1024,256]{1,0:T(8,128)(2,1)} fusion(bf16[2,512,256]{2,1,0:T(8,128)(2,1)S(1)} %copy.155, s32[1024]{0:T(1024)S(1)} %bitcast.231), kind=kCustom, calls=%fused_computation.1.clone | custom fusion | bytes 1056768 | tf_op jit(solution)/shard_map/jit(take_along_axis)/gather | solution.py:141
  214.4 4.9 add_convert_fusion
  223.2 22.8 %fusion = f32[2,4,64,2048]{3,2,1,0:T(8,128)} fusion(bf16[2,512,4,64]{1,3,2,0:T(8,128)(2,1)S(1)} %bitcast.246, f32[2,4,512,2048]{3,2,1,0:T(8,128)} %get-tuple-element.115, f32[2,4,512]{2,1,0:T(4,128)S(1)} %log_add_fusion, pred[2,2048]{1,0:T(4,128)(4,1)S(1)} %iota_compare_fusion), kind=kOutput, calls=%fused_computation.8 | convolution fusion | flops 6467616768 | bytes 38293504 | tf_op jit(solution)/shard_map/chqk,cqhd->ckhd/dot_general | solution.py:187
  246.0 16.6 %multiply_convert_fusion = bf16[2,4,512,2048]{3,2,1,0:T(8,128)(2,1)S(1)} fusion(f32[2,4,512,2048]{3,2,1,0:T(8,128)} %get-tuple-element.115, f32[2,4,512]{2,1,0:T(4,128)S(1)} %get-tuple-element.123, f32[2,4,512]{2,1,0:T(4,128)S(1)} %log_add_fusion, pred[2,2048]{1,0:T(4,128)(4,1)S(1)} %iota_compare_fusion, bf16[2,512,4,64]{1,3,2,0:T(8,128)(2,1)} %bitcast.247, ...), kind=kOutput, calls=%fused_computation.4 | convolution fusion | flops 1124073472 | bytes 52989952 | tf_op jit(solution)/shard_map/cqhd,ckhd->chqk/dot_general | solution.py:175
  262.7 5.6 %convolution_multiply_fusion = f32[2,4,64,2048]{3,2,1,0:T(8,128)} fusion(bf16[2,512,4,64]{1,3,2,0:T(8,128)(2,1)S(1)} %bitcast.237, bf16[2,4,512,2048]{3,2,1,0:T(8,128)(2,1)S(1)} %multiply_convert_fusion), kind=kOutput, calls=%fused_computation.42 | convolution fusion | flops 1074790400 | bytes 21495808 | tf_op jit(solution)/shard_map/chqk,cqhd->ckhd/dot_general | solution.py:184
  269.7 5.3 %copy.159 = f32[2,2048,256]{2,1,0:T(8,128)} copy(f32[2,2048,256]{1,2,0:T(8,128)} %bitcast.235) | data formatting | bytes 8388608 | tf_op jit(solution)/shard_map/reshape | solution.py:189
  275.0 5.3 %copy.160 = f32[2,2048,256]{2,1,0:T(8,128)} copy(f32[2,2048,256]{1,2,0:T(8,128)} %bitcast.238) | data formatting | bytes 8388608 | tf_op jit(solution)/shard_map/reshape | solution.py:189
  280.4 7.9 %pad_maximum_fusion = f32[2,2048,512]{2,1,0:T(8,128)} fusion(f32[2,2048,256]{2,1,0:T(8,128)} %copy.160, f32[2,2048,256]{2,1,0:T(8,128)} %copy.159), kind=kLoop, calls=%fused_computation.20 | loop fusion | flops 2097152 | bytes 16777216 | tf_op jit(solution)/shard_map/concatenate | solution.py:188
  288.3 12.5 %fusion.22 = bf16[2,4,64,512]{3,2,1,0:T(8,128)(2,1)} fusion(bf16[2,2048,4,64]{1,3,2,0:T(8,128)(2,1)} %bitcast.234, bf16[2,4,512,2048]{3,2,1,0:T(8,128)(2,1)} %copy-done.4), kind=kOutput, calls=%fused_computation.60 | convolution fusion | flops 1074266112 | bytes 19398656 | tf_op jit(solution)/shard_map/chqk,ckhd->cqhd/dot_general | solution.py:180
  303.0 2.3 convolution_bitcast_fusion.3
  305.3 3.4 convolution_bitcast_fusion
  310.5 50.6 %reduce-scatter.2.cloned.1.call-done = f32[2,512,512]{2,1,0:T(8,128)} async-done(((f32[2,2048,512]{2,1,0:T(8,128)}), f32[2,512,512]{2,1,0:T(8,128)}) %reduce-scatter.2.cloned.1.call-update) | async-done | bytes 2097168 | tf_op jit(solution)/shard_map/reduce_scatter | solution.py:192
  365.7 3.5 stack.30
  372.5 39.7 %all-reduce.3 = (f32[256]{0:T(256)}, f32[256]{0:T(256)}, f32[3,256]{1,0:T(4,128)}, f32[5]{0:T(128)S(1)}) all-reduce(f32[256]{0:T(256)S(1)} %get-tuple-element.75, f32[256]{0:T(256)S(1)} %get-tuple-element.80, f32[3,256]{1,0:T(4,128)S(1)} %convolution_bitcast_fusion.4, ...), channel_id=1, replica_groups=mesh['cells'=8,'slots'=4] {'cells','slots'}, use_global_device_ids=true, to_apply=%region_14.17 | all-reduce | flops 1285 | bytes 10280 | tf_op jit(solution)/shard_map/psum | solution.py:210
  417.1 2.7 add_add_fusion.2
  419.8 2.6 copy.169
  423.0 81.4 %all-reduce.7.cloned.1.call-done = (f32[256,768]{1,0:T(8,128)}, f32[256,256]{1,0:T(8,128)}, f32[256,1024]{1,0:T(8,128)}, f32[1024,256]{1,0:T(8,128)}) async-done(((f32[256,768]{1,0:T(8,128)}, f32[256,256]{1,0:T(8,128)}, f32[256,1024]{1,0:T(8,128)}, f32[1024,256]{1,0:T(8,128)}), (f32[256,768]{1,0:T(8,128)}, f32[256,256]{1,0:T(8,128)}, f32[256,1024]{1,0:T(8,128)}, ...) | async-done | bytes 3145744 | tf_op jit(solution)/shard_map/psum | solution.py:210
  508.2 2.3 copy.285
  (166 shorter events, 51.0 us)
Async XLA Ops:
  8.0 130.5 %copy-start = (bf16[256,1024]{1,0:T(8,128)(2,1)S(1)}, bf16[256,1024]{1,0:T(8,128)(2,1)}, u32[]{:S(2)}) copy-start(bf16[256,1024]{1,0:T(8,128)(2,1)} %param.24) | copy-start | bytes 1572868
  8.0 10.9 %sort.37.cloned.1.call-start = ((), (), s32[]{:S(2)}) async-start(), calls=%async_computation.6 | async-start | bytes 98336 | tf_op jit(solution)/shard_map/jit(argsort)/sort | solution.py:114
  10.1 52.2 %all-gather.2.cloned.1.call-start = ((), (), s32[]{:S(2)}) async-start(), calls=%async_computation.3 | async-start | bytes 5242880 | tf_op jit(solution)/shard_map/all_gather | solution.py:83
  11.5 5.6 %copy-start.35 = (s32[2]{0:T(128)S(1)}, s32[2]{0:T(128)}, u32[]{:S(2)}) copy-start(s32[2]{0:T(128)} %param.16) | copy-start | bytes 28
  11.5 9.5 %copy-start.2 = (s32[2,4,512]{2,1,0:T(4,128)S(1)}, s32[2,4,512]{2,1,0:T(4,128)}, u32[]{:S(2)}) copy-start(s32[2,4,512]{2,1,0:T(4,128)} %reshape.225) | copy-start | bytes 49156
  14.6 169.0 %sort.39.cloned.1.call-start = ((), (), s32[]{:S(2)}) async-start(), calls=%async_computation.7 | async-start | bytes 24608 | tf_op jit(solution)/shard_map/jit(argsort)/sort | solution.py:117
  21.1 40.3 %copy-start.33 = (s32[2,4,512]{2,1,0:T(4,128)S(1)}, s32[2,4,512]{2,1,0:T(4,128)}, u32[]{:S(2)}) copy-start(s32[2,4,512]{2,1,0:T(4,128)} %get-tuple-element.18) | copy-start | bytes 49156
  69.7 18.9 %copy-start.5 = (bf16[2,2048,256]{1,2,0:T(8,128)(2,1)}, bf16[2,2048,256]{1,2,0:T(8,128)(2,1)S(1)}, u32[]{:S(2)}) copy-start(bf16[2,2048,256]{1,2,0:T(8,128)(2,1)S(1)} %copy.142) | copy-start | bytes 6291460
  103.6 33.4 %copy-start.30 = (bf16[256,256]{1,0:T(8,128)(2,1)S(1)}, bf16[256,256]{1,0:T(8,128)(2,1)}, u32[]{:S(2)}) copy-start(bf16[256,256]{1,0:T(8,128)(2,1)} %param.22) | copy-start | bytes 393220
  140.4 10.5 %copy-start.16 = (f32[2,512,1024]{2,1,0:T(8,128)}, f32[2,512,1024]{2,1,0:T(8,128)S(1)}, u32[]{:S(2)}) copy-start(f32[2,512,1024]{2,1,0:T(8,128)S(1)} %get-tuple-element.119) | copy-start | bytes 12582916
  140.4 10.5 %copy-start.28 = (bf16[1024,256]{1,0:T(8,128)(2,1)S(1)}, bf16[1024,256]{1,0:T(8,128)(2,1)}, u32[]{:S(2)}) copy-start(bf16[1024,256]{1,0:T(8,128)(2,1)} %param.25) | copy-start | bytes 1572868
  152.8 21.7 %copy-start.3 = (s32[2,512]{1,0:T(2,128)S(1)}, s32[2,512]{1,0:T(2,128)}, u32[]{:S(2)}) copy-start(s32[2,512]{1,0:T(2,128)} %param.19) | copy-start | bytes 12292
  164.8 19.6 %copy-start.37 = (bf16[3,256]{1,0:T(4,128)(2,1)S(1)}, bf16[3,256]{1,0:T(4,128)(2,1)}, u32[]{:S(2)}) copy-start(bf16[3,256]{1,0:T(4,128)(2,1)} %param.26) | copy-start | bytes 4612
  170.2 14.2 %all-to-all-start = ((bf16[2,512,256]{2,0,1:T(2,128)(2,1)}), bf16[2,512,256]{2,0,1:T(2,128)(2,1)S(1)}, u32[]{:S(2)}, u32[]{:S(2)}) async-start(bf16[2,512,256]{2,0,1:T(2,128)(2,1)} %broadcast_select_fusion), calls=%async_computation | async-start | bytes 1048576 | tf_op jit(solution)/shard_map/all_to_all | solution.py:128
  184.4 8.4 %copy-start.20 = (bf16[2,512,256]{2,0,1:T(2,128)(2,1)}, bf16[2,512,256]{2,0,1:T(2,128)(2,1)S(1)}, u32[]{:S(2)}) copy-start(bf16[2,512,256]{2,0,1:T(2,128)(2,1)S(1)} %all-to-all-done) | copy-start | bytes 1572868
  187.9 13.1 %all-to-all-start.1 = ((bf16[2,512,256]{2,0,1:T(2,128)(2,1)}), bf16[2,512,256]{2,0,1:T(2,128)(2,1)}, u32[]{:S(2)}, u32[]{:S(2)}) async-start(bf16[2,512,256]{2,0,1:T(2,128)(2,1)} %copy.154), calls=%async_computation.1 | async-start | bytes 1048576 | tf_op jit(solution)/shard_map/all_to_all | solution.py:138
  192.1 169.0 %reduce-scatter.2.cloned.1.call-start = ((), (), s32[]{:S(2)}) async-start(), calls=%async_computation.4 | async-start | bytes 10485760 | tf_op jit(solution)/shard_map/reduce_scatter | solution.py:192
  214.4 7.3 %copy-start.10 = (bf16[2,512,256]{1,2,0:T(8,128)(2,1)}, bf16[2,512,256]{1,2,0:T(8,128)(2,1)S(1)}, u32[]{:S(2)}) copy-start(bf16[2,512,256]{1,2,0:T(8,128)(2,1)S(1)} %copy.156) | copy-start | bytes 1572868
  222.8 23.1 %copy-start.13 = (bf16[2,512,256]{1,2,0:T(8,128)(2,1)}, bf16[2,512,256]{1,2,0:T(8,128)(2,1)S(1)}, u32[]{:S(2)}) copy-start(bf16[2,512,256]{1,2,0:T(8,128)(2,1)S(1)} %fusion.37) | copy-start | bytes 1572868
  223.2 22.8 %copy-start.29 = (bf16[2,512,256]{1,2,0:T(8,128)(2,1)}, bf16[2,512,256]{1,2,0:T(8,128)(2,1)S(1)}, u32[]{:S(2)}) copy-start(bf16[2,512,256]{1,2,0:T(8,128)(2,1)S(1)} %get-tuple-element.124) | copy-start | bytes 1572868
  246.0 16.7 %copy-start.9 = (bf16[2,512,256]{1,2,0:T(8,128)(2,1)S(1)}, bf16[2,512,256]{1,2,0:T(8,128)(2,1)}, u32[]{:S(2)}) copy-start(bf16[2,512,256]{1,2,0:T(8,128)(2,1)} %copy.141) | copy-start | bytes 1572868
  262.6 7.1 %copy-start.4 = (bf16[2,4,512,2048]{3,2,1,0:T(8,128)(2,1)}, bf16[2,4,512,2048]{3,2,1,0:T(8,128)(2,1)S(1)}, u32[]{:S(2)}) copy-start(bf16[2,4,512,2048]{3,2,1,0:T(8,128)(2,1)S(1)} %multiply_convert_fusion) | copy-start | bytes 50331652
  288.3 14.7 %copy-start.14 = (bf16[2,512,256]{1,2,0:T(8,128)(2,1)S(1)}, bf16[2,512,256]{1,2,0:T(8,128)(2,1)}, u32[]{:S(2)}) copy-start(bf16[2,512,256]{1,2,0:T(8,128)(2,1)} %copy-done.13) | copy-start | bytes 1572868
  288.3 17.0 %copy-start.11 = (bf16[2,512,256]{1,2,0:T(8,128)(2,1)S(1)}, bf16[2,512,256]{1,2,0:T(8,128)(2,1)}, u32[]{:S(2)}) copy-start(bf16[2,512,256]{1,2,0:T(8,128)(2,1)} %copy-done.10) | copy-start | bytes 1572868
  288.3 216.1 %all-reduce.7.cloned.1.call-start = ((), (), s32[]{:S(2)}) async-start(), calls=%async_computation.5 | async-start | bytes 6291456 | tf_op jit(solution)/shard_map/psum | solution.py:210
  303.0 5.7 %copy-start.18 = (bf16[2,512,1024]{2,1,0:T(8,128)(2,1)S(1)}, bf16[2,512,1024]{2,1,0:T(8,128)(2,1)}, u32[]{:S(2)}) copy-start(bf16[2,512,1024]{2,1,0:T(8,128)(2,1)} %copy-done.17) | copy-start | bytes 6291460
  308.7 55.1 %copy-start.31 = (bf16[2,512,256]{2,1,0:T(8,128)(2,1)S(1)}, bf16[2,512,256]{2,1,0:T(8,128)(2,1)}, u32[]{:S(2)}) copy-start(bf16[2,512,256]{2,1,0:T(8,128)(2,1)} %copy.161) | copy-start | bytes 1572868
  308.7 55.1 %copy-start.36 = (f32[256]{0:T(256)S(1)}, f32[256]{0:T(256)}, u32[]{:S(2)}) copy-start(f32[256]{0:T(256)} %param.20) | copy-start | bytes 3076
  365.3 51.7 %copy-start.7 = (f32[2,512,256]{1,2,0:T(8,128)S(1)}, f32[2,512,256]{1,2,0:T(8,128)}, u32[]{:S(2)}) copy-start(f32[2,512,256]{1,2,0:T(8,128)} %copy-done.6) | copy-start | bytes 3145732
  365.3 51.7 %copy-start.12 = (bf16[2,512,256]{1,2,0:T(8,128)(2,1)S(1)}, bf16[2,512,256]{1,2,0:T(8,128)(2,1)}, u32[]{:S(2)}) copy-start(bf16[2,512,256]{1,2,0:T(8,128)(2,1)} %copy-done.10) | copy-start | bytes 1572868
  417.0 94.5 %copy-start.1 = (bf16[256,1024]{1,0:T(8,128)(2,1)S(1)}, bf16[256,1024]{1,0:T(8,128)(2,1)}, u32[]{:S(2)}) copy-start(bf16[256,1024]{1,0:T(8,128)(2,1)} %param.24) | copy-start | bytes 1572868
  504.4 6.1 %copy-start.27 = (f32[1024,256]{1,0:T(8,128)S(1)}, f32[1024,256]{1,0:T(8,128)}, u32[]{:S(2)}) copy-start(f32[1024,256]{1,0:T(8,128)} %get-tuple-element.133) | copy-start | bytes 3145732
  (14 other events, 37.5 us)
Sparse Core Ops, SparseCore 0:
  11.9 6.7 sort.41.cloned.1.call-done
  62.4 3.3 sort.43.cloned.1.call-done
  365.4 138.9 all-reduce.6
  (2 shorter events, 0.0 us)
Sparse Core Ops, SparseCore 1:
  14.7 37.0 all-gather.1
  288.4 72.7 reduce-scatter.1
where the time goes:
time: 529 us; the launch traced here: 519 us
  waiting for transfers between devices  140 us (26%)
  matrix products  131 us (25%)
  local copies, waits for them, and re-layouts  130 us (25%)
  other arithmetic  48.9 us (9%)
  blocking collectives  39.7 us (8%)
  between operations  20.2 us (4%)
  starting transfers between devices  8.51 us (2%)
    psum x1, waiting for transfers between devices, per_device(): lax.psum((grad_w_qkv, grad_w_out, grad_w_up, grad_w_down, grad_w_decoder,...  81.4 us
    reduce_scatter x1, waiting for transfers between devices, per_device(): lax.psum_scatter(grad_kv_all, 'slots', scatter_dimension=1, tiled=True)  50.6 us
    gather x2, local copies, waits for them, and re-layouts, per_device(): genes_sorted = jnp.take_along_axis(grouped, places_sorted, axis=-1)  40.3 us
    psum x1, blocking collectives, per_device(): lax.psum((grad_w_qkv, grad_w_out, grad_w_up, grad_w_down, grad_w_decoder,...  39.7 us
    dot_general x1, matrix products, per_device(): jnp.einsum('chqk,ckhd->chqd', attention, value_rows, precision=HIGH_PRECI...  33.3 us
    dot_general x1, matrix products, per_device(): jnp.einsum('chqk,cqhd->ckhd', attention, grad_heads_f, precision=HIGH_PRE...  22.8 us
    dot_general x1, matrix products, per_device(): jnp.einsum('cqhd,ckhd->chqk', grad_heads, value_rows, preferred_element_t...  16.6 us
    unnamed x91, local copies, waits for them, and re-layouts  16.4 us
  transfers between devices with their start and end apart: 5, of which 3 were waited for; matrix products, arithmetic and copies ran while one was open for 18% of the time, Pallas kernels for 0%

commit v1 on v0

v1 whole, which is shorter than its diff:
```python
import functools
import math

import jax
import jax.numpy as jnp
from jax import lax
from jax.experimental import pallas as pl
from jax.experimental.pallas import tpu as pltpu
from jax.sharding import PartitionSpec as P

HEADS = 4
EPS = 1e-05
BF16 = jnp.bfloat16
F32 = jnp.float32
NN = (((1,), (0,)), ((), ()))
NT = (((1,), (1,)), ((), ()))
TN = (((0,), (0,)), ((), ()))
VMEM_LIMIT = 56 * 2**20
SCORE_BOUND = 60.0
ERFC_P = 0.325
ERFC_C = (
    -5.927487965082223e-05,
    0.18467549445148965,
    0.1708094188150158,
    0.2414269376514742,
    -0.07282782022580145,
    0.6147421737182138,
    -0.5684607599983035,
    0.5878333184067656,
    -0.15813953377061551,
)


def dot(a, b, dims):
    return lax.dot_general(a, b, dims, preferred_element_type=F32)


def call(kernel, out_shape, flops=0, moved=0, **kw):
    return pl.pallas_call(
        kernel,
        out_shape=out_shape,
        compiler_params=pltpu.CompilerParams(vmem_limit_bytes=VMEM_LIMIT),
        cost_estimate=pl.CostEstimate(flops=int(flops), bytes_accessed=int(moved), transcendentals=0),
        **kw,
    )


def sds(shape, dtype):
    return jax.ShapeDtypeStruct(shape, dtype)


def norm_parts(x):
    centred = x - jnp.mean(x, axis=-1, keepdims=True)
    rstd = lax.rsqrt(jnp.mean(centred * centred, axis=-1, keepdims=True) + EPS)
    return centred * rstd, rstd


def norm_back(gy, xhat, rstd, gain):
    gx = gy * gain
    first = jnp.mean(gx, axis=-1, keepdims=True)
    second = jnp.mean(gx * xhat, axis=-1, keepdims=True)
    return rstd * (gx - first - xhat * second)


def head_ones(width):
    rows = lax.broadcasted_iota(jnp.int32, (width, width), 0) // (width // HEADS)
    cols = lax.broadcasted_iota(jnp.int32, (width, width), 1) // (width // HEADS)
    return (rows == cols).astype(BF16)


def qkv_kernel(info_ref, x_ref, gain_ref, w_ref, n_ref, q_ref, k_ref, v_ref, top_ref):
    block, width = x_ref.shape
    i = pl.program_id(0)
    xhat, _ = norm_parts(x_ref[...].astype(F32))
    normed = (xhat * gain_ref[...]).astype(BF16)
    n_ref[...] = normed
    mixed = dot(normed, w_ref[...], NN).astype(BF16)
    place = info_ref[1 + i] + lax.broadcasted_iota(jnp.int32, (block, 1), 0)
    live = (place < info_ref[0]).astype(BF16)
    q = mixed[:, :width] * BF16((width // HEADS) ** -0.5)
    k = mixed[:, width : 2 * width] * live
    q_ref[...] = q
    k_ref[...] = k
    v_ref[...] = mixed[:, 2 * width :] * live
    ones = head_ones(width)
    qq = q.astype(F32)
    kk = k.astype(F32)
    top_ref[...] = jnp.zeros_like(top_ref)
    top_ref[0, 0:1, :] = jnp.max(dot((qq * qq).astype(BF16), ones, NN), axis=0, keepdims=True)
    top_ref[0, 1:2, :] = jnp.max(dot((kk * kk).astype(BF16), ones, NN), axis=0, keepdims=True)


def qkv(info, x, gain, w):
    rows, width = x.shape
    block = rows // 4
    row = pl.BlockSpec((block, width), lambda i: (i, 0))
    whole = lambda a: pl.BlockSpec(a.shape, lambda i: (0, 0))
    return call(
        qkv_kernel,
        [sds((rows, width), BF16)] * 4 + [sds((rows // block, 8, width), F32)],
        flops=6 * rows * width * width,
        moved=10 * rows * width,
        grid=(rows // block,),
        in_specs=[pl.BlockSpec(memory_space=pltpu.SMEM), row, whole(gain), whole(w)],
        out_specs=[row] * 4 + [pl.BlockSpec((1, 8, width), lambda i: (i, 0, 0))],
    )(info, x, gain, w)


def attend_kernel(info_ref, place_ref, q_ref, k_ref, v_ref, top_ref, o_ref, linv_ref, p_ref, va_ref):
    keys = k_ref.shape[0]
    pair = q_ref.shape[1]
    half = pair // 2
    lane = lax.broadcasted_iota(jnp.int32, (1, pair), 1)
    live = place_ref[...] < info_ref[0]

    @pl.when(pl.program_id(1) == 0)
    def _():
        v = v_ref[...]
        mask = jnp.transpose(jnp.broadcast_to(live.astype(F32), (pair, keys))).astype(BF16)
        va_ref[0] = jnp.where(lane < half, v, mask)
        va_ref[1] = jnp.where(lane < half, mask, v)

    q = q_ref[...]
    zero = jnp.zeros_like(q)
    qs = (jnp.where(lane < half, q, zero), jnp.where(lane < half, zero, q))
    top = jnp.max(top_ref[...], axis=0)
    bound = jnp.max(top[0:1] * top[1:2])
    plain = bound * 1.05 < SCORE_BOUND * SCORE_BOUND

    def finish(outs):
        up = jnp.where(lane < half, outs[0], outs[1])
        down = pltpu.roll(jnp.where(lane < half, outs[1], outs[0]), half, 1)
        inverse = 1.0 / down
        o_ref[...] = up * inverse
        linv_ref[...] = inverse

    @pl.when(plain)
    def _():
        outs = []
        for h in range(2):
            p = jnp.exp(dot(qs[h], k_ref[...], NT)).astype(BF16)
            p_ref[h] = p
            outs.append(dot(p, va_ref[h], NN))
        finish(outs)

    @pl.when(jnp.logical_not(plain))
    def _():
        outs = []
        for h in range(2):
            s = jnp.where(live, dot(qs[h], k_ref[...], NT), -1e30)
            p = jnp.exp(s - jnp.max(s, axis=1, keepdims=True)).astype(BF16)
            p_ref[h] = p
            outs.append(dot(p, va_ref[h], NN))
        finish(outs)


def attend(info, place, q, k, v, top, rows, block=256):
    keys, width = k.shape
    pair = 2 * (width // HEADS)
    pairs = HEADS // 2
    qspec = pl.BlockSpec((block, pair), lambda h, i: (i, h))
    kspec = pl.BlockSpec((keys, pair), lambda h, i: (0, h))
    return call(
        attend_kernel,
        [sds((rows, width), F32), sds((rows, width), F32), sds((HEADS, rows, keys), BF16)],
        flops=16 * rows * keys * width,
        moved=2 * HEADS * rows * keys,
        grid=(pairs, rows // block),
        in_specs=[
            pl.BlockSpec(memory_space=pltpu.SMEM),
            pl.BlockSpec((1, keys), lambda h, i: (0, 0)),
            qspec,
            kspec,
            kspec,
            pl.BlockSpec((top.shape[0], 8, pair), lambda h, i: (0, 0, h)),
        ],
        out_specs=[qspec, qspec, pl.BlockSpec((2, block, keys), lambda h, i: (h, i, 0))],
        scratch_shapes=[pltpu.VMEM((2, keys, pair), BF16)],
    )(info, place, q, k, v, top)


def attend_back_kernel(place_ref, info_ref, q_ref, do_ref, dl_ref, delta_ref, linv_ref, k_ref, v_ref, p_ref,
                       dq_ref, dk_ref, dv_ref, ak_ref, av_ref, *, chunk):
    keys, pair = k_ref.shape
    half = pair // 2
    i = pl.program_id(0)
    lane = lax.broadcasted_iota(jnp.int32, (1, pair), 1)

    @pl.when(i == 0)
    def _():
        ak_ref[...] = jnp.zeros_like(ak_ref)
        av_ref[...] = jnp.zeros_like(av_ref)

    q = q_ref[...]
    do = do_ref[...]
    dl = dl_ref[...]
    zero = jnp.zeros_like(do)
    dq = []
    for h in range(2):
        own = (lane < half) if h == 0 else (lane >= half)
        doh = jnp.where(own, do, zero)
        lo = h * half
        delta = delta_ref[:, lo : lo + 1]
        linv = linv_ref[:, lo : lo + 1]
        total = None
        for c in range(keys // chunk):
            cut = slice(c * chunk, (c + 1) * chunk)
            kc = k_ref[cut, :]
            pc = p_ref[h, :, cut]
            dp = dot(doh, v_ref[cut, :], NT)
            ds = (pc.astype(F32) * (dp * linv - delta)).astype(BF16)
            part = dot(ds, kc, NN)
            total = part if total is None else total + part
            av_ref[lo : lo + half, cut] += dot(dl[:, lo : lo + half], pc, TN)
            ak_ref[lo : lo + half, cut] += dot(q[:, lo : lo + half], ds, TN)
        dq.append(total)
    dq_ref[...] = (jnp.where(lane < half, dq[0], dq[1]) * half**-0.5).astype(BF16)

    @pl.when(i == pl.num_programs(0) - 1)
    def _():
        live = place_ref[...] < info_ref[0]
        dk_ref[...] = jnp.where(live, ak_ref[...], 0.0).astype(BF16)
        dv_ref[...] = jnp.where(live, av_ref[...], 0.0).astype(BF16)


def attend_back(which, place, info, q, do, dl, delta, linv, k, v, p, block=512, chunk=512):
    rows = do.shape[0]
    keys, width = k.shape
    pair = 2 * (width // HEADS)
    qspec = pl.BlockSpec((block, pair), lambda i: (i, which))
    kspec = pl.BlockSpec((keys, pair), lambda i: (0, which))
    tspec = pl.BlockSpec((pair, keys), lambda i: (0, 0))
    return call(
        functools.partial(attend_back_kernel, chunk=chunk),
        [sds((rows, pair), BF16), sds((pair, keys), BF16), sds((pair, keys), BF16)],
        flops=16 * rows * keys * width,
        moved=rows * keys * HEADS,
        grid=(rows // block,),
        in_specs=[
            pl.BlockSpec((1, keys), lambda i: (0, 0)),
            pl.BlockSpec(memory_space=pltpu.SMEM),
            qspec,
            qspec,
            qspec,
            qspec,
            qspec,
            kspec,
            kspec,
            pl.BlockSpec((2, block, keys), lambda i: (which, i, 0)),
        ],
        out_specs=[pl.BlockSpec((block, pair), lambda i: (i, 0)), tspec, tspec],
        scratch_shapes=[pltpu.VMEM((pair, keys), F32), pltpu.VMEM((pair, keys), F32)],
    )(place, info, q, do, dl, delta, linv, k, v, p)


def gelu_parts(x):
    z = jnp.abs(x) * math.sqrt(0.5)
    t = 1.0 / (1.0 + ERFC_P * z)
    poly = jnp.full_like(t, ERFC_C[-1])
    for c in ERFC_C[-2::-1]:
        poly = poly * t + c
    bell = jnp.exp(-(z * z))
    tail = 0.5 * poly * bell
    cdf = jnp.where(x >= 0, 1.0 - tail, tail)
    return x * cdf, cdf + x * (bell * (1.0 / math.sqrt(2.0 * math.pi)))


def gamma_parts(x):
    large = x > 16.0
    small = jnp.minimum(x, 16.0)
    w = small * (small + 7.0)
    a, b, c = w + 6.0, w + 10.0, w + 12.0
    log_prod = jnp.log(w * a * (b * c))
    sum_inv = (2.0 * small + 7.0) * (1.0 / w + 1.0 / a + 1.0 / b + 1.0 / c)
    big = jnp.where(large, x, x + 8.0)
    log_big = jnp.log(big)
    inv = 1.0 / big
    inv2 = inv * inv
    lg = (big - 0.5) * log_big - big + 0.5 * math.log(2.0 * math.pi)
    lg = lg + inv * (1.0 / 12.0 - inv2 * (1.0 / 360.0 - inv2 * (1.0 / 1260.0)))
    dg = log_big - 0.5 * inv - inv2 * (1.0 / 12.0 - inv2 * (1.0 / 120.0 - inv2 * (1.0 / 252.0)))
    return jnp.where(large, lg, lg - log_prod), jnp.where(large, dg, dg - sum_inv)


def softplus(x):
    return jnp.maximum(x, 0.0) + jnp.log(1.0 + jnp.exp(-jnp.abs(x)))


def sigmoid(x):
    return 1.0 / (1.0 + jnp.exp(-x))


def zinb(m, t, p, y, scale):
    rate = scale * (softplus(m) + 0.05)
    theta = softplus(t) + 0.05
    total = theta + rate
    inv_total = 1.0 / total
    log_total = jnp.log(total)
    log_theta = jnp.log(theta)
    z0 = theta * (log_theta - log_total)
    pi = sigmoid(p)
    e0 = jnp.exp(z0)
    den = pi + (1.0 - pi) * e0
    inv_den = 1.0 / den
    some = y > 0
    yf = y.astype(F32)
    lg_sum, dg_sum = gamma_parts(yf + theta)
    lg_theta, dg_theta = gamma_parts(theta)
    lg_y, _ = gamma_parts(yf + 1.0)
    log_nb = lg_sum - lg_theta - lg_y + z0 + yf * (jnp.log(rate) - log_total)
    nll = jnp.where(some, softplus(p) - log_nb, -jnp.log(den))
    g_z0 = jnp.where(some, -1.0, -(1.0 - pi) * e0 * inv_den)
    share = theta * inv_total
    g_theta = g_z0 * (log_theta - log_total + 1.0 - share)
    g_theta = g_theta + jnp.where(some, dg_theta - dg_sum + yf * inv_total, 0.0)
    g_rate = jnp.where(some, yf * (inv_total - 1.0 / rate), 0.0) - g_z0 * share
    g_p = jnp.where(some, pi, -(1.0 - e0) * inv_den * pi * (1.0 - pi))
    return nll, g_rate * scale * sigmoid(m), g_theta * sigmoid(t), g_p


def split2(x):
    high = x.astype(BF16)
    return high, (x - high.astype(F32)).astype(BF16)


def middle_kernel(info_ref, scale_ref, o_ref, linv_ref, x_ref, gain_ref, w_out_ref, w_up_ref, w_down_ref,
                  w_dec_ref, gene_ref, table_ref,
                  gres_ref, do_ref, dl_ref, delta_ref, g_down_ref, g_up_ref, g_out_ref, small_ref,
                  res_s, n2_s, act_s, gp_s, dec_s, gd_s, ga_down, ga_up, ga_out, *, block):
    rows, width = o_ref.shape
    hidden = w_up_ref.shape[1]
    length = rows // 2
    valid_len = info_ref[0]
    gain = gain_ref[...]
    small_ref[...] = jnp.zeros_like(small_ref)
    ga_down[...] = jnp.zeros_like(ga_down)
    ga_up[...] = jnp.zeros_like(ga_up)
    ga_out[...] = jnp.zeros_like(ga_out)

    def rowsum(a):
        return jnp.sum(a, axis=0, keepdims=True)

    for b in range(rows // block):
        cut = slice(b * block, (b + 1) * block)
        base = info_ref[1 + b * block // length] + b * block % length
        valid = (base + lax.broadcasted_iota(jnp.int32, (block, 1), 0) < valid_len).astype(F32)
        attn_out = dot(o_ref[cut].astype(BF16), w_out_ref[...], NN)
        resid = x_ref[cut].astype(F32) + attn_out
        res_s[cut] = resid
        xhat, _ = norm_parts(resid)
        normed = (xhat * gain).astype(BF16)
        n2_s[cut] = normed
        act, slope = gelu_parts(dot(normed, w_up_ref[...], NN))
        act = act.astype(BF16)
        act_s[cut] = act
        gp_s[cut] = slope
        mlp_out = dot(act, w_down_ref[...], NN)
        final = resid + mlp_out
        dec_s[cut] = final.astype(BF16)
        small_ref[0:1, :] += rowsum(valid * final * final)
        small_ref[1:2, :] += rowsum(valid * attn_out * attn_out)
        small_ref[2:3, :] += rowsum(valid * mlp_out * mlp_out)

    decoded = dot(w_dec_ref[...], dec_s[...], NT)
    gene = gene_ref[...]
    high = (lax.broadcasted_iota(jnp.int32, (table_ref.shape[0], rows), 0) == gene // 128).astype(BF16)
    found = dot(table_ref[...], high, TN)
    low = lax.broadcasted_iota(jnp.int32, (128, rows), 0) == gene % 128
    observed = rowsum(jnp.where(low, found, 0.0))
    places = lax.broadcasted_iota(jnp.int32, (1, rows), 1)
    places = jnp.where(places < length, info_ref[1] + places, info_ref[2] + places - length)
    valid = (places < valid_len).astype(F32)
    nll, g_m, g_t, g_p = zinb(decoded[0:1], decoded[1:2], decoded[2:3], observed, scale_ref[0])
    nll = nll * valid
    for j in range(rows // width):
        small_ref[3:4, :] += nll[:, j * width : (j + 1) * width]
        small_ref[4:5, :] += valid[:, j * width : (j + 1) * width]
    gd_s[...] = jnp.zeros_like(gd_s)
    for j, g in enumerate((g_m, g_t, g_p)):
        gh, gl = split2(g * valid)
        gd_s[j : j + 1, :] = gh.astype(F32)
        gd_s[3 + j : 4 + j, :] = gl.astype(F32)
    gd = gd_s[...].astype(BF16)
    gw = dot(gd, dec_s[...], NN)
    small_ref[5:8, :] = gw[0:3] + gw[3:6]
    w_dec = w_dec_ref[...].astype(F32)
    w_twice = jnp.concatenate([w_dec[0:3], w_dec[0:3], jnp.zeros((10, width), F32)], axis=0).astype(BF16)

    ones = head_ones(width)
    for b in range(rows // block):
        cut = slice(b * block, (b + 1) * block)
        g_final = dot(gd[:, cut], w_twice, TN).astype(BF16)
        ga_down[...] += dot(act_s[cut], g_final, TN)
        g_up = (dot(g_final, w_down_ref[...], NT) * gp_s[cut]).astype(BF16)
        ga_up[...] += dot(n2_s[cut], g_up, TN)
        g_normed = dot(g_up, w_up_ref[...], NT)
        xhat, rstd = norm_parts(res_s[cut])
        small_ref[8:9, :] += rowsum(g_normed * xhat)
        g_res = g_final.astype(F32) + norm_back(g_normed, xhat, rstd, gain)
        gres_ref[cut] = g_res
        g_attn = g_res.astype(BF16)
        o = o_ref[cut]
        linv = linv_ref[cut]
        ga_out[...] += dot(o.astype(BF16), g_attn, TN)
        do = dot(g_attn, w_out_ref[...], NT).astype(BF16)
        do_ref[cut] = do
        dof = do.astype(F32)
        dl_ref[cut] = (dof * linv).astype(BF16)
        ph, pl_ = split2(dof * o)
        delta_ref[cut] = (dot(ph, ones, NN) + dot(pl_, ones, NN)) * linv

    g_down_ref[...] = ga_down[...].astype(BF16)
    for j in range(hidden // width):
        g_up_ref[j * width : (j + 1) * width, :] = ga_up[:, j * width : (j + 1) * width].astype(BF16)
    g_out_ref[...] = ga_out[...].astype(BF16)


def middle(info, scale, o, linv, x, gain, w_out, w_up, w_down, w_dec, gene, table, block=256):
    rows, width = o.shape
    hidden = w_up.shape[1]
    smem = pl.BlockSpec(memory_space=pltpu.SMEM)
    vmem = pl.BlockSpec(memory_space=pltpu.VMEM)
    return call(
        functools.partial(middle_kernel, block=block),
        [
            sds((rows, width), F32),
            sds((rows, width), BF16),
            sds((rows, width), BF16),
            sds((rows, width), F32),
            sds((hidden, width), BF16),
            sds((hidden, width), BF16),
            sds((width, width), BF16),
            sds((16, width), F32),
        ],
        flops=12 * rows * width * hidden,
        moved=20 * rows * width,
        in_specs=[smem, smem] + [vmem] * 10,
        out_specs=[vmem] * 8,
        scratch_shapes=[
            pltpu.VMEM((rows, width), F32),
            pltpu.VMEM((rows, width), BF16),
            pltpu.VMEM((rows, hidden), BF16),
            pltpu.VMEM((rows, hidden), F32),
            pltpu.VMEM((rows, width), BF16),
            pltpu.VMEM((16, rows), F32),
            pltpu.VMEM((hidden, width), F32),
            pltpu.VMEM((width, hidden), F32),
            pltpu.VMEM((width, width), F32),
        ],
    )(info, scale, o, linv, x, gain, w_out, w_up, w_down, w_dec, gene, table)


def last_kernel(x_ref, n_ref, gain_ref, w_ref, dq0_ref, dq1_ref, dk0_ref, dk1_ref, dv0_ref, dv1_ref,
                g_ref, gain_out_ref, own_ref, send_ref, *, block):
    keys, width = x_ref.shape
    rows = dq0_ref.shape[0]
    pair = dq0_ref.shape[1]
    n_own = n_ref[:rows]
    n_all = n_ref[...]
    for j, (dq, dk, dv) in enumerate(((dq0_ref, dk0_ref, dv0_ref), (dq1_ref, dk1_ref, dv1_ref))):
        cut = slice(j * pair, (j + 1) * pair)
        g_ref[0:width, cut] = dot(n_own, dq[...], TN).astype(BF16)
        g_ref[width : 2 * width, cut] = jnp.transpose(dot(dk[...], n_all, NN)).astype(BF16)
        g_ref[2 * width :, cut] = jnp.transpose(dot(dv[...], n_all, NN)).astype(BF16)
    total = jnp.zeros((1, width), F32)
    w = w_ref[...]
    for b in range(keys // block):
        cut = slice(b * block, (b + 1) * block)
        gn = jnp.zeros((block, width), F32)
        for j, (dq, dk, dv) in enumerate(((dq0_ref, dk0_ref, dv0_ref), (dq1_ref, dk1_ref, dv1_ref))):
            lo = j * pair
            if b * block < rows:
                gn += dot(dq[cut], w[:, lo : lo + pair], NT)
            tt = (((0,), (1,)), ((), ()))
            gn += dot(dk[:, cut], w[:, width + lo : width + lo + pair], tt)
            gn += dot(dv[:, cut], w[:, 2 * width + lo : 2 * width + lo + pair], tt)
        xhat, _ = norm_parts(x_ref[cut].astype(F32))
        total += jnp.sum(gn * xhat, axis=0, keepdims=True)
        if b * block < rows:
            own_ref[cut] = gn
        else:
            send_ref[b * block - rows : (b + 1) * block - rows] = gn.astype(BF16)
    gain_out_ref[...] = jnp.broadcast_to(total, gain_out_ref.shape)


def last(x, n, gain, w, dq, dk, dv, block=512):
    keys, width = x.shape
    rows = dq[0].shape[0]
    vmem = pl.BlockSpec(memory_space=pltpu.VMEM)
    return call(
        functools.partial(last_kernel, block=block),
        [sds((3 * width, width), BF16), sds((8, width), F32), sds((rows, width), F32), sds((keys - rows, width), BF16)],
        flops=12 * keys * width * width,
        moved=16 * keys * width,
        in_specs=[vmem] * 10,
        out_specs=[vmem] * 4,
    )(x, n, gain, w, dq[0], dq[1], dk[0], dk[1], dv[0], dv[1])


def tokens_kernel(x_ref, gain_ref, gres_ref, own_ref, got_ref, mine_ref, back_ref):
    length = mine_ref.shape[0]
    for b in range(2):
        cut = slice(b * length, (b + 1) * length)
        xhat, rstd = norm_parts(x_ref[cut].astype(F32))
        gn = own_ref[cut] + got_ref[cut].astype(F32)
        g = gres_ref[cut] + norm_back(gn, xhat, rstd, gain_ref[...])
        if b == 0:
            mine_ref[...] = g
        else:
            back_ref[...] = g.astype(BF16)


def tokens_back(x, gain, gres, own, got):
    rows, width = gres.shape
    vmem = pl.BlockSpec(memory_space=pltpu.VMEM)
    return call(
        tokens_kernel,
        [sds((rows // 2, width), F32), sds((rows // 2, width), BF16)],
        flops=30 * rows * width,
        moved=12 * rows * width,
        in_specs=[vmem] * 5,
        out_specs=[vmem] * 2,
    )(x, gain, gres, own, got)


def swap(x, axis, bit):
    size = lax.axis_size(axis)
    return lax.ppermute(x, axis, [(i, i ^ bit) for i in range(size)])


def split3(x):
    high = lax.reduce_precision(x, 8, 7)
    rest = x - high
    mid = lax.reduce_precision(rest, 8, 7)
    return jnp.concatenate([high, mid, rest - mid], axis=0).astype(BF16)


def join3(x):
    n = x.shape[0] // 3
    x = x.astype(F32)
    return x[:n] + x[n : 2 * n] + x[2 * n :]


def total_over_devices(main, small):
    steps = []
    for axis in ("slots", "cells"):
        bit = 1
        while bit < lax.axis_size(axis):
            steps.append((axis, bit))
            bit *= 2
    halving, rest = steps[:1] + steps[2:3], steps[1:2] + steps[3:]
    for axis, bit in halving:
        side = (lax.axis_index(axis) // bit) % 2
        n = main.shape[0] // 2
        keep = lax.dynamic_slice_in_dim(main, side * n, n, 0)
        send = lax.dynamic_slice_in_dim(main, (1 - side) * n, n, 0)
        got = swap(jnp.concatenate([send, split3(small)], axis=0), axis, bit)
        main = (keep.astype(F32) + got[:n].astype(F32)).astype(BF16)
        small = small + join3(got[n:])
    for axis, bit in rest:
        n = main.shape[0]
        got = swap(jnp.concatenate([main, split3(small)], axis=0), axis, bit)
        main = (main.astype(F32) + got[:n].astype(F32)).astype(BF16)
        small = small + join3(got[n:])
    for axis, bit in halving[::-1]:
        side = (lax.axis_index(axis) // bit) % 2
        got = swap(main, axis, bit)
        main = jnp.where(side == 0, jnp.concatenate([main, got], 0), jnp.concatenate([got, main], 0))
    return main, small


def per_device(
    tokens,
    valid_len,
    library,
    gene_slot,
    counts,
    norm1_gain,
    w_qkv,
    w_out,
    norm2_gain,
    w_up,
    w_down,
    w_decoder,
):
    cells, length, width = tokens.shape
    hidden = w_up.shape[1]
    slots = lax.axis_size("slots")
    me = lax.axis_index("slots")
    cell = me // 2
    pick = lambda a: lax.dynamic_index_in_dim(a, cell, 0, keepdims=False)
    other = lambda a: lax.dynamic_index_in_dim(a, 1 - cell, 0, keepdims=False)

    came = swap(other(tokens), "slots", 2)
    own = jnp.concatenate([pick(tokens), came], axis=0)
    x = jnp.concatenate([own, swap(own, "slots", 1)], axis=0)
    came_counts = swap(other(counts), "slots", 2)
    two = jnp.stack([pick(counts), came_counts])
    two_more = swap(two, "slots", 1)
    table = jnp.stack([two[0], two_more[0], two[1], two_more[1]]).reshape(-1, 128).astype(BF16)

    blocks = jnp.stack([me, me ^ 2, me ^ 1, me ^ 3]).astype(jnp.int32)
    info = jnp.concatenate([pick(valid_len)[None], blocks * length])
    place = (blocks[:, None] * length + jnp.arange(length, dtype=jnp.int32)[None]).reshape(1, -1)
    scale = (pick(library).astype(F32) / (slots * length))[None]
    gene = pick(gene_slot).reshape(slots, length)
    gene = jnp.stack([lax.dynamic_index_in_dim(gene, b, 0, keepdims=False) for b in (me, me ^ 2)])
    gene = (((gene // length) ^ me) * length + gene % length).reshape(1, -1)

    gain1 = norm1_gain[None]
    gain2 = norm2_gain[None]
    w_dec = jnp.concatenate([w_decoder, jnp.zeros((13, width), BF16)], axis=0)

    rows = 2 * length
    n, q, k, v, top = qkv(info, x, gain1, w_qkv)
    o, linv, p = attend(info, place, q, k, v, top, rows)
    gres, do, dl, delta, g_down, g_up, g_out, small = middle(
        info, scale, o, linv, x, gain2, w_out, w_up, w_down, w_dec, gene, table
    )
    back = [attend_back(h, place, info, q, do, dl, delta, linv, k, v, p) for h in range(HEADS // 2)]
    g_qkv, g_gain1, gn_own, gn_send = last(
        x, n, gain1, w_qkv, [b[0] for b in back], [b[1] for b in back], [b[2] for b in back]
    )
    gn_got = swap(gn_send, "slots", 1)
    mine, away = tokens_back(x, gain1, gres, gn_own, gn_got)
    returned = swap(away, "slots", 2).astype(F32)
    grad_tokens = jnp.where(cell == 0, jnp.stack([mine, returned]), jnp.stack([returned, mine]))

    main = jnp.concatenate([g_down, g_up, g_out, g_qkv], axis=0)
    small = jnp.concatenate([small[:9], g_gain1[:1]], axis=0)
    main, small = total_over_devices(main, small)
    main = main.astype(F32)
    at = 0
    parts = []
    for size in (hidden, hidden, width, 3 * width):
        parts.append(main[at : at + size])
        at += size
    unstack = lambda a: jnp.concatenate(list(a.reshape(-1, width, width)), axis=1)
    sums = jnp.sum(small, axis=1)
    count = sums[4]
    summary = jnp.stack(
        [
            sums[3] / count,
            jnp.sqrt(sums[0] / (count * width)),
            jnp.sqrt(sums[1] / (count * width)),
            jnp.sqrt(sums[2] / (count * width)),
        ]
    )
    return (
        grad_tokens,
        small[9],
        unstack(parts[3]),
        parts[2],
        small[8],
        unstack(parts[1]),
        parts[0],
        small[5:8],
        summary,
    )


def solution(mesh):
    in_specs = (
        P("cells", "slots", None),
        P("cells"),
        P("cells"),
        P("cells", None),
        P("cells", "slots"),
        P(),
        P(),
        P(),
        P(),
        P(),
        P(),
        P(),
    )
    out_specs = (P("cells", "slots", None), P(), P(), P(), P(), P(), P(), P(), P())
    return jax.shard_map(
        per_device, mesh=mesh, in_specs=in_specs, out_specs=out_specs, check_vma=False
    )
```

time: 529 us -> 163 us (0.31); the launches traced: 519 us -> 162 us
  matrix products: 131 us -> 0 us
  local copies, waits for them, and re-layouts: 130 us -> 11.2 us
  waiting for transfers between devices: 140 us -> 49.8 us
  Pallas kernels: 0 us -> 70.6 us
  blocking collectives: 39.7 us -> 0 us
  other arithmetic: 48.9 us -> 9.25 us
  between operations: 20.2 us -> 5.82 us
  starting transfers between devices: 8.51 us -> 15.3 us
    dot_general x21 -> x0, matrix products: 131 us -> none  [the longest x1 33.3 us: per_device(): jnp.einsum('chqk,ckhd->chqd', attention, value_rows, precision=HIGH_PRECI...]
    psum x1 -> x0, waiting for transfers between devices: 81.4 us -> none  [per_device(): lax.psum((grad_w_qkv, grad_w_out, grad_w_up, grad_w_down, grad_w_decoder,...]
    gather x7 -> x0, local copies, waits for them, and re-layouts: 72.4 us -> none  [the longest x2 40.3 us: per_device(): genes_sorted = jnp.take_along_axis(grouped, places_sorted, axis=-1)]
    pallas_call x0 -> x7, Pallas kernels: none -> 70.6 us  [the longest x2 24.9 us: attend_back(): call(functools.partial(attend_back_kernel, chunk=chunk), [sds((rows, pair...]
    reduce_scatter x1 -> x0, waiting for transfers between devices: 50.6 us -> none  [per_device(): lax.psum_scatter(grad_kv_all, 'slots', scatter_dimension=1, tiled=True)]
    ppermute x0 -> x13, waiting for transfers between devices: none -> 49.8 us  [swap(): return lax.ppermute(x, axis, [(i, i ^ bit) for i in range(size)])]
    psum x1 -> x0, blocking collectives: 39.7 us -> none  [per_device(): lax.psum((grad_w_qkv, grad_w_out, grad_w_up, grad_w_down, grad_w_decoder,...]
    reduce_sum x7 -> x1, other arithmetic: 17.1 us -> 0.12 us  [per_device(): sums = jnp.sum(small, axis=1)]
  transfers between devices with their start and end apart: 5 -> 13, of which waited for: 3 -> 7; matrix products, arithmetic and copies ran while one was open for 18% -> 6% of each run, Pallas kernels for 0% -> 2%
where the time goes in v1:
time: 163 us; the launch traced here: 162 us
  Pallas kernels  70.6 us (43%)
  waiting for transfers between devices  49.8 us (31%)
  starting transfers between devices  15.3 us (9%)
  local copies, waits for them, and re-layouts  11.2 us (7%)
  other arithmetic  9.25 us (6%)
  between operations  5.82 us (4%)
    ppermute x13, waiting for transfers between devices, swap(): return lax.ppermute(x, axis, [(i, i ^ bit) for i in range(size)])  49.8 us
    pallas_call x2, Pallas kernels, attend_back(): call(functools.partial(attend_back_kernel, chunk=chunk), [sds((rows, pair...  24.9 us
    pallas_call x1, Pallas kernels, attend(): call(attend_kernel, [sds((rows, width), F32), sds((rows, width), F32), sd...  16.1 us
    ppermute x13, starting transfers between devices, swap(): return lax.ppermute(x, axis, [(i, i ^ bit) for i in range(size)])  15.3 us
    pallas_call x1, Pallas kernels, middle(): call(functools.partial(middle_kernel, block=block), [sds((rows, width), F...  15 us
    pallas_call x1, Pallas kernels, last(): call(functools.partial(last_kernel, block=block), [sds((3 * width, width)...  6.05 us
    pallas_call x1, Pallas kernels, qkv(): call(qkv_kernel, [sds((rows, width), BF16)] * 4 + [sds((rows // block, 8,...  5.02 us
    pallas_call x1, Pallas kernels, tokens_back(): call(tokens_kernel, [sds((rows // 2, width), F32), sds((rows // 2, width)...  3.45 us
  transfers between devices with their start and end apart: 13, of which 7 were waited for; matrix products, arithmetic and copies ran while one was open for 6% of the time, Pallas kernels for 2%

profile of v1, /device:TPU:0, one launch (start us, length us, event | category | flops | bytes accessed | tf_op | source)
XLA Modules:
  0.0 161.8 jit_solution(13759341279366126042)
XLA Ops:
  0.7 1.1 dynamic-slice_bitcast_fusion.1
  1.8 3.0 %collective-permute-start = (bf16[512,256]{1,0:T(8,128)(2,1)S(1)}, bf16[512,256]{1,0:T(8,128)(2,1)S(1)}, u32[]{:S(2)}, u32[]{:S(2)}) collective-permute-start(bf16[512,256]{1,0:T(8,128)(2,1)S(1)} %get-tuple-element.86), channel_id=1, source_target_pairs={{0,2},{1,3},{2,0},{3,1},{4,6},{5,7},{6,4},{7,5},{8,10},{9,11},{10,... | collective-permute-start | bytes 786440 | tf_op jit(solution)/shard_map/ppermute | solution.py:528
  4.8 0.8 fusion.18
  6.5 1.2 dynamic_slice.46
  7.8 3.3 %collective-permute-done = bf16[512,256]{1,0:T(8,128)(2,1)S(1)} collective-permute-done((bf16[512,256]{1,0:T(8,128)(2,1)S(1)}, bf16[512,256]{1,0:T(8,128)(2,1)S(1)}, u32[]{:S(2)}, u32[]{:S(2)}) %collective-permute-start) | collective-permute-done | bytes 262176 | tf_op jit(solution)/shard_map/ppermute | solution.py:528
  11.8 1.2 pad_add_fusion.1.info_ref
  16.2 1.0 pad_maximum_fusion.x_ref
  17.2 5.0 %shard_map.187 = (bf16[2048,256]{1,0:T(8,128)(2,1)}, bf16[2048,256]{1,0:T(8,128)(2,1)}, bf16[2048,256]{1,0:T(8,128)(2,1)}, bf16[2048,256]{1,0:T(8,128)(2,1)}, f32[4,8,256]{2,1,0:T(8,128)}) custom-call(s32[5]{0:T(128)} %pad_add_fusion.1.info_ref, bf16[2048,256]{1,0:T(8,128)(2,1)} %pad_maximum_fusion.x_ref, f32[1,256]{1,0:T(1,128)} %bitcast.39, ...), custom_call_target="tpu_custom_call" | custom-call | flops 805306368 | bytes 5242880 | tf_op jit(solution)/shard_map/pallas_call | solution.py:98
  22.2 16.1 %shard_map.188 = (f32[1024,256]{1,0:T(8,128)}, f32[1024,256]{1,0:T(8,128)}, bf16[4,1024,2048]{2,1,0:T(8,128)(2,1)}) custom-call(s32[5]{0:T(128)} %pad_add_fusion.1.info_ref, s32[1,2048]{1,0:T(1,128)} %bitcast.31, bf16[2048,256]{1,0:T(8,128)(2,1)} %get-tuple-element.37.q_ref, bf16[2048,256]{1,0:T(8,128)(2,1)} %get-tuple-element.38.k_ref, ...), custom_call_target="tpu_custom_call" | custom-call | flops 8589934592 | bytes 16777216 | tf_op jit(solution)/shard_map/pallas_call | solution.py:163
  38.4 15.0 %shard_map.189 = (f32[1024,256]{1,0:T(8,128)}, bf16[1024,256]{1,0:T(8,128)(2,1)}, bf16[1024,256]{1,0:T(8,128)(2,1)}, f32[1024,256]{1,0:T(8,128)}, bf16[1024,256]...) custom-call(s32[5]{0:T(128)} %pad_add_fusion.1.info_ref, ...), custom_call_target="tpu_custom_call" | custom-call | flops 3221225472 | bytes 5242880 | tf_op jit(solution)/shard_map/pallas_call | solution.py:423
  53.4 12.6 %shard_map.191 = (bf16[1024,128]{1,0:T(8,128)(2,1)}, bf16[128,2048]{1,0:T(8,128)(2,1)}, bf16[128,2048]{1,0:T(8,128)(2,1)}) custom-call(s32[1,2048]{1,0:T(1,128)} %bitcast.32, s32[5]{0:T(128)} %pad_add_fusion.1.info_ref, bf16[2048,256]{1,0:T(8,128)(2,1)} %get-tuple-element.37.q_ref, bf16[1024,256]{1,0:T(8,128)(2,1)} %get-tuple-element.45.do_ref, ...), custom_call_target="tpu_custom_call" | custom-call | flops 8589934592 | bytes 8388608 | tf_op jit(solution)/shard_map/pallas_call | solution.py:233
  66.0 12.3 %shard_map.190 = (bf16[1024,128]{1,0:T(8,128)(2,1)}, bf16[128,2048]{1,0:T(8,128)(2,1)}, bf16[128,2048]{1,0:T(8,128)(2,1)}) custom-call(s32[1,2048]{1,0:T(1,128)} %bitcast.33, s32[5]{0:T(128)} %pad_add_fusion.1.info_ref, bf16[2048,256]{1,0:T(8,128)(2,1)} %get-tuple-element.37.q_ref, bf16[1024,256]{1,0:T(8,128)(2,1)} %get-tuple-element.45.do_ref, ...), custom_call_target="tpu_custom_call" | custom-call | flops 8589934592 | bytes 8388608 | tf_op jit(solution)/shard_map/pallas_call | solution.py:233
  78.3 6.0 %shard_map.192 = (bf16[768,256]{1,0:T(8,128)(2,1)}, f32[8,256]{1,0:T(8,128)}, f32[1024,256]{1,0:T(8,128)}, bf16[1024,256]{1,0:T(8,128)(2,1)}) custom-call(bf16[2048,256]{1,0:T(8,128)(2,1)} %pad_maximum_fusion.x_ref, bf16[2048,256]{1,0:T(8,128)(2,1)} %get-tuple-element.44.n_ref, f32[1,256]{1,0:T(1,128)} %bitcast.40, bf16[256,768]{1,0:T(8,128)(2,1)} %w_ref.3, ...), custom_call_target="tpu_custom_call" | custom-call | flops 1610612736 | bytes 8388608 | tf_op jit(solution)/shard_map/pallas_call | solution.py:490
  86.4 2.3 %collective-permute-done.6 = bf16[1566,256]{1,0:T(8,128)(2,1)S(1)} collective-permute-done((bf16[1566,256]{1,0:T(8,128)(2,1)S(1)}, bf16[1566,256]{1,0:T(8,128)(2,1)S(1)}, u32[]{:S(2)}, u32[]{:S(2)}) %collective-permute-start.6) | collective-permute-done | bytes 801824 | tf_op jit(solution)/shard_map/ppermute | solution.py:528
  89.0 1.8 %collective-permute-start.7 = (bf16[798,256]{1,0:T(8,128)(2,1)S(1)}, bf16[798,256]{1,0:T(8,128)(2,1)S(1)}, u32[]{:S(2)}, u32[]{:S(2)}) collective-permute-start(bf16[798,256]{1,0:T(8,128)(2,1)S(1)} %pad_maximum_fusion.4), channel_id=1, source_target_pairs={{0,4},{4,0},{8,12},{12,8},{16,20},{20,16},{24,28},{28,24},{1,5},{5... | collective-permute-start | bytes 1225736 | tf_op jit(solution)/shard_map/ppermute | solution.py:528
  90.8 9.8 %collective-permute-done.7 = bf16[798,256]{1,0:T(8,128)(2,1)S(1)} collective-permute-done((bf16[798,256]{1,0:T(8,128)(2,1)S(1)}, bf16[798,256]{1,0:T(8,128)(2,1)S(1)}, u32[]{:S(2)}, u32[]{:S(2)}) %collective-permute-start.7) | collective-permute-done | bytes 408608 | tf_op jit(solution)/shard_map/ppermute | solution.py:528
  100.8 1.8 %collective-permute-start.8 = (bf16[798,256]{1,0:T(8,128)(2,1)S(1)}, bf16[798,256]{1,0:T(8,128)(2,1)S(1)}, u32[]{:S(2)}, u32[]{:S(2)}) collective-permute-start(bf16[798,256]{1,0:T(8,128)(2,1)S(1)} %pad_maximum_fusion.5), channel_id=1, source_target_pairs={{0,2},{1,3},{2,0},{3,1},{4,6},{5,7},{6,4},{7,5},{8,10},{9,11},{10,... | collective-permute-start | bytes 1225736 | tf_op jit(solution)/shard_map/ppermute | solution.py:528
  102.6 9.0 %collective-permute-done.8 = bf16[798,256]{1,0:T(8,128)(2,1)S(1)} collective-permute-done((bf16[798,256]{1,0:T(8,128)(2,1)S(1)}, bf16[798,256]{1,0:T(8,128)(2,1)S(1)}, u32[]{:S(2)}, u32[]{:S(2)}) %collective-permute-start.8) | collective-permute-done | bytes 408608 | tf_op jit(solution)/shard_map/ppermute | solution.py:528
  111.8 1.9 %collective-permute-start.9 = (bf16[798,256]{1,0:T(8,128)(2,1)S(1)}, bf16[798,256]{1,0:T(8,128)(2,1)S(1)}, u32[]{:S(2)}, u32[]{:S(2)}) collective-permute-start(bf16[798,256]{1,0:T(8,128)(2,1)S(1)} %pad_maximum_fusion.6), channel_id=1, source_target_pairs={{0,8},{4,12},{8,0},{12,4},{16,24},{20,28},{24,16},{28,20},{1,9},{5... | collective-permute-start | bytes 1225736 | tf_op jit(solution)/shard_map/ppermute | solution.py:528
  113.6 8.0 %collective-permute-done.9 = bf16[798,256]{1,0:T(8,128)(2,1)S(1)} collective-permute-done((bf16[798,256]{1,0:T(8,128)(2,1)S(1)}, bf16[798,256]{1,0:T(8,128)(2,1)S(1)}, u32[]{:S(2)}, u32[]{:S(2)}) %collective-permute-start.9) | collective-permute-done | bytes 408608 | tf_op jit(solution)/shard_map/ppermute | solution.py:528
  121.8 2.8 %collective-permute-start.10 = (bf16[798,256]{1,0:T(8,128)(2,1)S(1)}, bf16[798,256]{1,0:T(8,128)(2,1)S(1)}, u32[]{:S(2)}, u32[]{:S(2)}) collective-permute-start(bf16[798,256]{1,0:T(8,128)(2,1)S(1)} %pad_maximum_fusion.7), channel_id=1, source_target_pairs={{0,16},{4,20},{8,24},{12,28},{16,0},{20,4},{24,8},{28,12},{1,17},{... | collective-permute-start | bytes 1225736 | tf_op jit(solution)/shard_map/ppermute | solution.py:528
  124.7 0.8 copy-done.4
  125.5 3.4 %shard_map.193 = (f32[512,256]{1,0:T(8,128)}, bf16[512,256]{1,0:T(8,128)(2,1)}) custom-call(bf16[2048,256]{1,0:T(8,128)(2,1)} %pad_maximum_fusion.x_ref, f32[1,256]{1,0:T(1,128)} %bitcast.41, f32[1024,256]{1,0:T(8,128)} %get-tuple-element.43.gres_ref, f32[1024,256]{1,0:T(8,128)} %get-tuple-element.55.own_ref, bf16[1024,256]{1,0:T(8,128)(2,1)} %copy-done.4), custom_call_target="tpu_custom_call" | custom-call | flops 7864320 | bytes 3145728 | tf_op jit(solution)/shard_map/pallas_call | solution.py:516
  128.9 1.5 collective-permute-start.5
  130.4 10.1 %collective-permute-done.10 = bf16[798,256]{1,0:T(8,128)(2,1)S(1)} collective-permute-done((bf16[798,256]{1,0:T(8,128)(2,1)S(1)}, bf16[798,256]{1,0:T(8,128)(2,1)S(1)}, u32[]{:S(2)}, u32[]{:S(2)}) %collective-permute-start.10) | collective-permute-done | bytes 408608 | tf_op jit(solution)/shard_map/ppermute | solution.py:528
  140.6 1.6 collective-permute-start.11
  142.3 1.0 maximum_select_fusion.1
  143.3 7.3 %collective-permute-done.11 = bf16[768,256]{1,0:T(8,128)(2,1)S(1)} collective-permute-done((bf16[768,256]{1,0:T(8,128)(2,1)S(1)}, bf16[768,256]{1,0:T(8,128)(2,1)S(1)}, u32[]{:S(2)}, u32[]{:S(2)}) %collective-permute-start.11) | collective-permute-done | bytes 393248 | tf_op jit(solution)/shard_map/ppermute | solution.py:528
  157.9 0.9 fusion.19
  158.8 1.0 slice.204
  159.8 0.9 pad_maximum_fusion.2
  160.7 1.1 pad_maximum_fusion.1
  (90 shorter events, 10.2 us)
Async XLA Ops:
  0.6 5.0 %copy-start = (s32[2,2048]{1,0:T(2,128)S(1)}, s32[2,2048]{1,0:T(2,128)}, u32[]{:S(2)}) copy-start(s32[2,2048]{1,0:T(2,128)} %param.15) | copy-start | bytes 49156
  0.7 13.0 %copy-start.10 = (s32[2]{0:T(128)S(1)}, s32[2]{0:T(128)}, u32[]{:S(2)}) copy-start(s32[2]{0:T(128)} %param.14) | copy-start | bytes 28
  0.7 14.2 %copy-start.8 = (bf16[3,256]{1,0:T(4,128)(2,1)S(1)}, bf16[3,256]{1,0:T(4,128)(2,1)}, u32[]{:S(2)}) copy-start(bf16[3,256]{1,0:T(4,128)(2,1)} %param.23) | copy-start | bytes 4612
  1.8 9.4 %collective-permute-start = (bf16[512,256]{1,0:T(8,128)(2,1)S(1)}, bf16[512,256]{1,0:T(8,128)(2,1)S(1)}, u32[]{:S(2)}, u32[]{:S(2)}) collective-permute-start(bf16[512,256]{1,0:T(8,128)(2,1)S(1)} %get-tuple-element.86), channel_id=1, source_target_pairs={{0,2},{1,3},{2,0},{3,1},{4,6},{5,7},{6,4},{7,5},{8,10},{9,11},{10,... | collective-permute-start | bytes 786440 | tf_op jit(solution)/shard_map/ppermute | solution.py:528
  5.6 5.7 %collective-permute-start.2 = (s32[512]{0:T(512)S(1)}, s32[512]{0:T(512)S(1)}, u32[]{:S(2)}, u32[]{:S(2)}) collective-permute-start(s32[512]{0:T(512)S(1)} %bitcast.36), channel_id=1, source_target_pairs={{0,2},{1,3},{2,0},{3,1},{4,6},{5,7},{6,4},{7,5},{8,10},{9,11},{10,... | collective-permute-start | bytes 6152 | tf_op jit(solution)/shard_map/ppermute | solution.py:528
  11.2 5.0 %collective-permute-start.1 = (bf16[1024,256]{1,0:T(8,128)(2,1)S(1)}, bf16[1024,256]{1,0:T(8,128)(2,1)S(1)}, u32[]{:S(2)}, u32[]{:S(2)}) collective-permute-start(bf16[1024,256]{1,0:T(8,128)(2,1)S(1)} %pad_maximum_fusion.3), channel_id=1, source_target_pairs={{0,1},{1,0},{2,3},{3,2},{4,5},{5,4},{6,7},{7,6},{8,9},{9,8},{10,11... | collective-permute-start | bytes 1572872 | tf_op jit(solution)/shard_map/ppermute | solution.py:528
  11.3 4.2 %collective-permute-start.3 = (s32[2,512]{1,0:T(2,128)S(1)}, s32[2,512]{1,0:T(2,128)S(1)}, u32[]{:S(2)}, u32[]{:S(2)}) collective-permute-start(s32[2,512]{1,0:T(2,128)S(1)} %pad_add_fusion), channel_id=1, source_target_pairs={{0,1},{1,0},{2,3},{3,2},{4,5},{5,4},{6,7},{7,6},{8,9},{9,8},{10,11... | collective-permute-start | bytes 12296 | tf_op jit(solution)/shard_map/ppermute | solution.py:528
  78.3 6.8 %copy-start.3 = (bf16[1024,256]{1,0:T(8,128)(2,1)S(1)}, bf16[1024,256]{1,0:T(8,128)(2,1)}, u32[]{:S(2)}) copy-start(bf16[1024,256]{1,0:T(8,128)(2,1)} %get-tuple-element.61) | copy-start | bytes 1572868
  78.3 6.9 %copy-start.7 = (f32[16,256]{1,0:T(8,128)S(1)}, f32[16,256]{1,0:T(8,128)}, u32[]{:S(2)}) copy-start(f32[16,256]{1,0:T(8,128)} %get-tuple-element.59) | copy-start | bytes 49156
  78.3 6.9 %copy-start.2 = (bf16[1024,256]{1,0:T(8,128)(2,1)S(1)}, bf16[1024,256]{1,0:T(8,128)(2,1)}, u32[]{:S(2)}) copy-start(bf16[1024,256]{1,0:T(8,128)(2,1)} %get-tuple-element.62) | copy-start | bytes 1572868
  84.4 0.9 copy-start.6
  84.4 1.1 copy-start.5
  86.3 2.4 %collective-permute-start.6 = (bf16[1566,256]{1,0:T(8,128)(2,1)S(1)}, bf16[1566,256]{1,0:T(8,128)(2,1)S(1)}, u32[]{:S(2)}, u32[]{:S(2)}) collective-permute-start(bf16[1566,256]{1,0:T(8,128)(2,1)S(1)} %concatenate.77), channel_id=1, source_target_pairs={{0,1},{1,0},{2,3},{3,2},{4,5},{5,4},{6,7},{7,6},{8,9},{9,8},{10,11... | collective-permute-start | bytes 2405384 | tf_op jit(solution)/shard_map/ppermute | solution.py:528
  89.0 11.6 %collective-permute-start.7 = (bf16[798,256]{1,0:T(8,128)(2,1)S(1)}, bf16[798,256]{1,0:T(8,128)(2,1)S(1)}, u32[]{:S(2)}, u32[]{:S(2)}) collective-permute-start(bf16[798,256]{1,0:T(8,128)(2,1)S(1)} %pad_maximum_fusion.4), channel_id=1, source_target_pairs={{0,4},{4,0},{8,12},{12,8},{16,20},{20,16},{24,28},{28,24},{1,5},{5... | collective-permute-start | bytes 1225736 | tf_op jit(solution)/shard_map/ppermute | solution.py:528
  100.8 12.9 %copy-start.9 = (bf16[1024,256]{1,0:T(8,128)(2,1)S(1)}, bf16[1024,256]{1,0:T(8,128)(2,1)}, u32[]{:S(2)}) copy-start(bf16[1024,256]{1,0:T(8,128)(2,1)} %get-tuple-element.56) | copy-start | bytes 1572868
  100.8 10.7 %collective-permute-start.8 = (bf16[798,256]{1,0:T(8,128)(2,1)S(1)}, bf16[798,256]{1,0:T(8,128)(2,1)S(1)}, u32[]{:S(2)}, u32[]{:S(2)}) collective-permute-start(bf16[798,256]{1,0:T(8,128)(2,1)S(1)} %pad_maximum_fusion.5), channel_id=1, source_target_pairs={{0,2},{1,3},{2,0},{3,1},{4,6},{5,7},{6,4},{7,5},{8,10},{9,11},{10,... | collective-permute-start | bytes 1225736 | tf_op jit(solution)/shard_map/ppermute | solution.py:528
  111.8 9.9 %collective-permute-start.9 = (bf16[798,256]{1,0:T(8,128)(2,1)S(1)}, bf16[798,256]{1,0:T(8,128)(2,1)S(1)}, u32[]{:S(2)}, u32[]{:S(2)}) collective-permute-start(bf16[798,256]{1,0:T(8,128)(2,1)S(1)} %pad_maximum_fusion.6), channel_id=1, source_target_pairs={{0,8},{4,12},{8,0},{12,4},{16,24},{20,28},{24,16},{28,20},{1,9},{5... | collective-permute-start | bytes 1225736 | tf_op jit(solution)/shard_map/ppermute | solution.py:528
  113.6 11.0 %collective-permute-start.4 = (bf16[1024,256]{1,0:T(8,128)(2,1)S(1)}, bf16[1024,256]{1,0:T(8,128)(2,1)S(1)}, u32[]{:S(2)}, u32[]{:S(2)}) collective-permute-start(bf16[1024,256]{1,0:T(8,128)(2,1)S(1)} %copy-done.9), channel_id=1, source_target_pairs={{0,1},{1,0},{2,3},{3,2},{4,5},{5,4},{6,7},{7,6},{8,9},{9,8},{10,11... | collective-permute-start | bytes 1572872 | tf_op jit(solution)/shard_map/ppermute | solution.py:528
  121.8 18.7 %collective-permute-start.10 = (bf16[798,256]{1,0:T(8,128)(2,1)S(1)}, bf16[798,256]{1,0:T(8,128)(2,1)S(1)}, u32[]{:S(2)}, u32[]{:S(2)}) collective-permute-start(bf16[798,256]{1,0:T(8,128)(2,1)S(1)} %pad_maximum_fusion.7), channel_id=1, source_target_pairs={{0,16},{4,20},{8,24},{12,28},{16,0},{20,4},{24,8},{28,12},{1,17},{... | collective-permute-start | bytes 1225736 | tf_op jit(solution)/shard_map/ppermute | solution.py:528
  124.7 0.8 copy-start.4
  128.9 13.4 %copy-start.1 = (f32[512,256]{1,0:T(8,128)S(1)}, f32[512,256]{1,0:T(8,128)}, u32[]{:S(2)}) copy-start(f32[512,256]{1,0:T(8,128)} %get-tuple-element.57) | copy-start | bytes 1572868
  128.9 13.3 %collective-permute-start.5 = (bf16[512,256]{1,0:T(8,128)(2,1)}, bf16[512,256]{1,0:T(8,128)(2,1)S(1)}, u32[]{:S(2)}, u32[]{:S(2)}) collective-permute-start(bf16[512,256]{1,0:T(8,128)(2,1)} %get-tuple-element.58), channel_id=1, source_target_pairs={{0,2},{1,3},{2,0},{3,1},{4,6},{5,7},{6,4},{7,5},{8,10},{9,11},{10,... | collective-permute-start | bytes 786440 | tf_op jit(solution)/shard_map/ppermute | solution.py:528
  140.6 10.0 %collective-permute-start.11 = (bf16[768,256]{1,0:T(8,128)(2,1)S(1)}, bf16[768,256]{1,0:T(8,128)(2,1)S(1)}, u32[]{:S(2)}, u32[]{:S(2)}) collective-permute-start(bf16[768,256]{1,0:T(8,128)(2,1)S(1)} %add_convert_fusion.1), channel_id=1, source_target_pairs={{0,4},{4,0},{8,12},{12,8},{16,20},{20,16},{24,28},{28,24},{1,5},{5... | collective-permute-start | bytes 1179656 | tf_op jit(solution)/shard_map/ppermute | solution.py:528
  150.9 6.6 %collective-permute-start.12 = (bf16[1536,256]{1,0:T(8,128)(2,1)S(1)}, bf16[1536,256]{1,0:T(8,128)(2,1)S(1)}, u32[]{:S(2)}, u32[]{:S(2)}) collective-permute-start(bf16[1536,256]{1,0:T(8,128)(2,1)S(1)} %maximum_select_fusion.2), channel_id=1, source_target_pairs={{0,1},{1,0},{2,3},{3,2},{4,5},{5,4},{6,7},{7,6},{8,9},{9,8},{10,11... | collective-permute-start | bytes 2359304 | tf_op jit(solution)/shard_map/ppermute | solution.py:528

commit v2 on v1

v2 whole, which is shorter than its diff:
```python
import functools
import math

import jax
import jax.numpy as jnp
from jax import lax
from jax.experimental import pallas as pl
from jax.experimental.pallas import tpu as pltpu
from jax.sharding import PartitionSpec as P

HEADS = 4
EPS = 1e-05
BF16 = jnp.bfloat16
F32 = jnp.float32
NN = (((1,), (0,)), ((), ()))
NT = (((1,), (1,)), ((), ()))
TN = (((0,), (0,)), ((), ()))
SCORE_BOUND = 60.0
ERFC_P = 0.325
ERFC_C = (
    -5.927487965082223e-05,
    0.18467549445148965,
    0.1708094188150158,
    0.2414269376514742,
    -0.07282782022580145,
    0.6147421737182138,
    -0.5684607599983035,
    0.5878333184067656,
    -0.15813953377061551,
)


def dot(a, b, dims):
    return lax.dot_general(a, b, dims, preferred_element_type=F32)


def call(kernel, out_shape, flops=0, moved=0, vmem=48, **kw):
    return pl.pallas_call(
        kernel,
        out_shape=out_shape,
        compiler_params=pltpu.CompilerParams(vmem_limit_bytes=vmem * 2**20),
        cost_estimate=pl.CostEstimate(flops=int(flops), bytes_accessed=int(moved), transcendentals=0),
        **kw,
    )


def sds(shape, dtype):
    return jax.ShapeDtypeStruct(shape, dtype)


def norm_parts(x):
    centred = x - jnp.mean(x, axis=-1, keepdims=True)
    rstd = lax.rsqrt(jnp.mean(centred * centred, axis=-1, keepdims=True) + EPS)
    return centred * rstd, rstd


def norm_back(gy, xhat, rstd, gain):
    gx = gy * gain
    first = jnp.mean(gx, axis=-1, keepdims=True)
    second = jnp.mean(gx * xhat, axis=-1, keepdims=True)
    return rstd * (gx - first - xhat * second)


def head_ones(width, lanes=None, step=None):
    rows = lax.broadcasted_iota(jnp.int32, (width, lanes or width), 0) // (width // HEADS)
    cols = lax.broadcasted_iota(jnp.int32, (width, lanes or width), 1) // (step or width // HEADS)
    return (rows == cols).astype(F32).astype(BF16)


def live_rows(me_ref, len_ref, block, length):
    place = (me_ref[0] ^ block) * length + lax.broadcasted_iota(jnp.int32, (length, 1), 0)
    return place < len_ref[me_ref[0] // 2]


def qkv_kernel(me_ref, len_ref, own_ref, pair_ref, gain_ref, w_ref, n_out, q_ref, k_ref, v_ref, top_ref, n_ref, n_sem, *, first):
    length, width = pair_ref.shape
    ones = head_ones(width)
    top_ref[...] = jnp.zeros_like(top_ref)
    for j in range(2):
        cut = slice(j * length, (j + 1) * length)
        if j == 1:
            x = pair_ref[...]
        elif first == 0:
            x = own_ref[me_ref[0] // 2]
        else:
            x = own_ref[...]
        xhat, _ = norm_parts(x.astype(F32))
        normed = (xhat * gain_ref[...]).astype(BF16)
        n_ref[cut] = normed
        live = live_rows(me_ref, len_ref, first + j, length).astype(F32).astype(BF16)
        skip = width if j == 1 else 0
        mixed = dot(normed, w_ref[:, skip:], NN).astype(BF16)
        if j == 0:
            q = mixed[:, :width] * BF16((width // HEADS) ** -0.5)
            q_ref[...] = q
            qf = q.astype(F32)
            top_ref[0:1, :] = jnp.max(dot((qf * qf).astype(BF16), ones, NN), axis=0, keepdims=True)
        k = mixed[:, width - skip : 2 * width - skip] * live
        k_ref[cut] = k
        v_ref[cut] = mixed[:, 2 * width - skip :] * live
        kf = k.astype(F32)
        top_ref[1 + j : 2 + j, :] = jnp.max(dot((kf * kf).astype(BF16), ones, NN), axis=0, keepdims=True)
    keep_n = pltpu.make_async_copy(n_ref, n_out, n_sem)
    keep_n.start()
    if first == 0:
        keep_n.wait()


def qkv(me, valid_len, own, pair, gain, w, first):
    length, width = pair.shape
    smem = pl.BlockSpec(memory_space=pltpu.SMEM)
    vmem = pl.BlockSpec(memory_space=pltpu.VMEM)
    hbm = pl.BlockSpec(memory_space=pltpu.HBM)
    rows = 2 * length
    return call(
        functools.partial(qkv_kernel, first=first),
        [
            pltpu.HBM((rows, width), BF16),
            sds((length, width), BF16),
            sds((rows, width), BF16),
            sds((rows, width), BF16),
            sds((8, width), F32),
        ],
        flops=6 * rows * width * width,
        moved=10 * rows * width,
        vmem=16,
        in_specs=[smem, smem] + [vmem] * 4,
        out_specs=[hbm] + [vmem] * 4,
        scratch_shapes=[pltpu.VMEM((rows, width), BF16), pltpu.SemaphoreType.DMA],
    )(me, valid_len, own, pair, gain, w)


def live_keys(me_ref, len_ref, keys):
    lane = lax.broadcasted_iota(jnp.int32, (1, keys), 1)
    length = keys // 4
    place = ((lane // length) ^ me_ref[0]) * length + lane % length
    return place < len_ref[me_ref[0] // 2]


def gelu_parts(x):
    z = jnp.abs(x) * math.sqrt(0.5)
    t = 1.0 / (1.0 + ERFC_P * z)
    poly = jnp.full_like(t, ERFC_C[-1])
    for c in ERFC_C[-2::-1]:
        poly = poly * t + c
    bell = jnp.exp(-(z * z))
    tail = 0.5 * poly * bell
    cdf = jnp.where(x >= 0, 1.0 - tail, tail)
    return x * cdf, cdf + x * (bell * (1.0 / math.sqrt(2.0 * math.pi)))


def gamma_parts(x):
    large = x > 16.0
    small = jnp.minimum(x, 16.0)
    w = small * (small + 7.0)
    a, b, c = w + 6.0, w + 10.0, w + 12.0
    log_prod = jnp.log(w * a * (b * c))
    sum_inv = (2.0 * small + 7.0) * (1.0 / w + 1.0 / a + 1.0 / b + 1.0 / c)
    big = jnp.where(large, x, x + 8.0)
    log_big = jnp.log(big)
    inv = 1.0 / big
    inv2 = inv * inv
    lg = (big - 0.5) * log_big - big + 0.5 * math.log(2.0 * math.pi)
    lg = lg + inv * (1.0 / 12.0 - inv2 * (1.0 / 360.0 - inv2 * (1.0 / 1260.0)))
    dg = log_big - 0.5 * inv - inv2 * (1.0 / 12.0 - inv2 * (1.0 / 120.0 - inv2 * (1.0 / 252.0)))
    return jnp.where(large, lg, lg - log_prod), jnp.where(large, dg, dg - sum_inv)


def softplus(x):
    return jnp.maximum(x, 0.0) + jnp.log(1.0 + jnp.exp(-jnp.abs(x)))


def sigmoid(x):
    return 1.0 / (1.0 + jnp.exp(-x))


def zinb(m, t, p, y, scale):
    rate = scale * (softplus(m) + 0.05)
    theta = softplus(t) + 0.05
    total = theta + rate
    inv_total = 1.0 / total
    log_total = jnp.log(total)
    log_theta = jnp.log(theta)
    z0 = theta * (log_theta - log_total)
    pi = sigmoid(p)
    e0 = jnp.exp(z0)
    den = pi + (1.0 - pi) * e0
    inv_den = 1.0 / den
    some = y > 0
    yf = y.astype(F32)
    lg_sum, dg_sum = gamma_parts(yf + theta)
    lg_theta, dg_theta = gamma_parts(theta)
    lg_y, _ = gamma_parts(yf + 1.0)
    log_nb = lg_sum - lg_theta - lg_y + z0 + yf * (jnp.log(rate) - log_total)
    nll = jnp.where(some, softplus(p) - log_nb, -jnp.log(den))
    g_z0 = jnp.where(some, -1.0, -(1.0 - pi) * e0 * inv_den)
    share = theta * inv_total
    g_theta = g_z0 * (log_theta - log_total + 1.0 - share)
    g_theta = g_theta + jnp.where(some, dg_theta - dg_sum + yf * inv_total, 0.0)
    g_rate = jnp.where(some, yf * (inv_total - 1.0 / rate), 0.0) - g_z0 * share
    g_p = jnp.where(some, pi, -(1.0 - e0) * inv_den * pi * (1.0 - pi))
    return nll, g_rate * scale * sigmoid(m), g_theta * sigmoid(t), g_p


def split2(x):
    high = x.astype(BF16)
    return high, (x - high.astype(F32)).astype(BF16)


def layer_kernel(me_ref, len_ref, lib_ref, xa_ref, xb_ref, pb_ref, gain1_ref, w_ref, qa_ref, ka_ref, va_ref, ta_ref,
                 gain_ref, w_out_ref, w_up_ref, w_down_ref, w_dec_ref, gene_ref, c0_ref, c1_ref, c2_ref, c3_ref,
                 p_ref, nb_ref, gres_out, keep_out, qb_ref, kb_ref, vb_ref, tb_ref, do_ref, dl_ref, cols_ref, send_ref,
                 small_ref,
                 nb_s, nb_sem, gres_ref, keep_ref, out_sem, q_s, x_s, p_s, p_sem, gt_s, aug_s, o_s, linv_s, res_s, n2_s, act_s, gp_s, dec_s, gd_s, w_s, table_s, ga_down, ga_up, ga_out,
                 *, block):
    part, width = ka_ref.shape
    keys = 2 * part
    length = part // 2
    rows = part
    hidden = w_up_ref.shape[1]
    pair = 2 * (width // HEADS)
    half = pair // 2
    pairs = HEADS // 2
    me = me_ref[0]
    cell = me // 2
    valid_len = len_ref[cell]
    gain = gain_ref[...]
    small_ref[...] = jnp.zeros_like(small_ref)
    ga_down[...] = jnp.zeros_like(ga_down)
    ga_up[...] = jnp.zeros_like(ga_up)
    ga_out[...] = jnp.zeros_like(ga_out)
    lane = lax.broadcasted_iota(jnp.int32, (1, pair), 1)

    def rowsum(a):
        return jnp.sum(a, axis=0, keepdims=True)

    qkv_kernel(me_ref, len_ref, xb_ref, pb_ref, gain1_ref, w_ref, nb_ref, qb_ref, kb_ref, vb_ref, tb_ref, nb_s, nb_sem, first=2)

    live = live_keys(me_ref, len_ref, keys)
    mask = jnp.transpose(jnp.broadcast_to(live.astype(F32), (pair, keys))).astype(BF16)
    for j, ref in enumerate((va_ref, vb_ref)):
        cut = slice(j * part, (j + 1) * part)
        for g in range(pairs):
            v = ref[:, g * pair : (g + 1) * pair]
            aug_s[2 * g, cut] = jnp.where(lane < half, v, mask[cut])
            aug_s[2 * g + 1, cut] = jnp.where(lane < half, mask[cut], v)

    top_q = jnp.maximum(ta_ref[0:1], tb_ref[0:1])
    top_k = jnp.maximum(jnp.maximum(ta_ref[1:2], tb_ref[1:2]), jnp.maximum(ta_ref[2:3], tb_ref[2:3]))
    plain = jnp.max(top_q * top_k) * 1.05 < SCORE_BOUND * SCORE_BOUND

    q_s[0:length] = qa_ref[...]
    q_s[length:rows] = qb_ref[...]
    x_s[0:length] = xa_ref[cell]
    x_s[length:rows] = xb_ref[...]

    def copy(b, g):
        slot = (b * pairs + g) % 2
        return pltpu.make_async_copy(
            p_s.at[slot], p_ref.at[pl.ds(2 * g, 2), pl.ds(pl.multiple_of(b * block, block), block)], p_sem.at[slot]
        )

    def attend_block(b, g, safe):
        cut = pl.ds(pl.multiple_of(b * block, block), block)
        cols = slice(g * pair, (g + 1) * pair)
        slot = (b * pairs + g) % 2
        q = q_s[cut, cols]
        zero = jnp.zeros_like(q)
        outs = []
        for h in range(2):
            qh = jnp.where(lane < half, q, zero) if h == 0 else jnp.where(lane < half, zero, q)
            if safe:
                s = jnp.concatenate([dot(qh, ref[:, cols], NT) for ref in (ka_ref, kb_ref)], axis=1)
                s = jnp.where(live, s, -1e30)
                p = jnp.exp(s - jnp.max(s, axis=1, keepdims=True)).astype(BF16)
                p_s[slot, h] = p
                total = dot(p, aug_s[2 * g + h], NN)
            else:
                total = None
                for j, ref in enumerate((ka_ref, kb_ref)):
                    kcut = slice(j * part, (j + 1) * part)
                    p = jnp.exp(dot(qh, ref[:, cols], NT)).astype(BF16)
                    p_s[slot, h, :, kcut] = p
                    o = dot(p, aug_s[2 * g + h, kcut], NN)
                    total = o if total is None else total + o
            outs.append(total)
        up = jnp.where(lane < half, outs[0], outs[1])
        down = pltpu.roll(jnp.where(lane < half, outs[1], outs[0]), half, 1)
        inverse = 1.0 / down
        o_s[cut, cols] = up * inverse
        linv_s[cut, cols] = inverse

    @pl.loop(0, rows // block)
    def _(b):
        for g in range(pairs):

            @pl.when(b > 0)
            def _():
                copy(b - 1, g).wait()

            pl.when(plain)(functools.partial(attend_block, b, g, False))
            pl.when(jnp.logical_not(plain))(functools.partial(attend_block, b, g, True))
            copy(b, g).start()

    @pl.loop(0, rows // block)
    def _(b):
        start = pl.multiple_of(b * block, block)
        cut = pl.ds(start, block)
        base = jnp.where(start < length, me * length + start, (me ^ 2) * length + start - length)
        valid = (base + lax.broadcasted_iota(jnp.int32, (block, 1), 0) < valid_len).astype(F32)
        attn_out = dot(o_s[cut].astype(BF16), w_out_ref[...], NN)
        resid = x_s[cut].astype(F32) + attn_out
        res_s[cut] = resid
        xhat, _ = norm_parts(resid)
        normed = (xhat * gain).astype(BF16)
        n2_s[cut] = normed
        act, slope = gelu_parts(dot(normed, w_up_ref[...], NN))
        act = act.astype(BF16)
        act_s[cut] = act
        gp_s[cut] = slope
        mlp_out = dot(act, w_down_ref[...], NN)
        final = resid + mlp_out
        dec_s[cut] = final.astype(BF16)
        small_ref[0:1, :] += rowsum(valid * final * final)
        small_ref[1:2, :] += rowsum(valid * attn_out * attn_out)
        small_ref[2:3, :] += rowsum(valid * mlp_out * mlp_out)

    w_s[...] = jnp.zeros_like(w_s)
    w_s[0:3, :] = w_dec_ref[...].astype(F32)
    w_s[3:6, :] = w_dec_ref[...].astype(F32)
    w_twice = w_s[...].astype(BF16)
    decoded = dot(w_twice, dec_s[...], NT)
    for j, ref in enumerate((c0_ref, c1_ref, c2_ref, c3_ref)):
        for i in range(length // 128):
            table_s[j * (length // 128) + i : j * (length // 128) + i + 1, :] = ref[:, i * 128 : (i + 1) * 128].astype(F32)
    starts = (me * length, (me ^ 2) * length)
    gene = jnp.concatenate([gene_ref[pl.ds(cell, 1), pl.ds(pl.multiple_of(a, length), length)] for a in starts], axis=1)
    gene = ((gene // length) ^ me) * length + gene % length
    high = (lax.broadcasted_iota(jnp.int32, (table_s.shape[0], rows), 0) == gene // 128).astype(F32).astype(BF16)
    found = dot(table_s[...].astype(BF16), high, TN)
    low = lax.broadcasted_iota(jnp.int32, (128, rows), 0) == gene % 128
    observed = rowsum(jnp.where(low, found, 0.0))
    lane = lax.broadcasted_iota(jnp.int32, (1, rows), 1)
    places = jnp.where(lane < length, starts[0] + lane, starts[1] + lane - length)
    valid = (places < valid_len).astype(F32)
    scale = lib_ref[cell].astype(F32) / (4 * length)
    nll, g_m, g_t, g_p = zinb(decoded[0:1], decoded[1:2], decoded[2:3], observed, scale)
    nll = nll * valid
    for j in range(rows // width):
        small_ref[3:4, :] += nll[:, j * width : (j + 1) * width]
        small_ref[4:5, :] += valid[:, j * width : (j + 1) * width]
    gd_s[...] = jnp.zeros_like(gd_s)
    for j, g in enumerate((g_m, g_t, g_p)):
        gh, gl = split2(g * valid)
        gd_s[j : j + 1, :] = gh.astype(F32)
        gd_s[3 + j : 4 + j, :] = gl.astype(F32)
    gd = gd_s[...].astype(BF16)
    gw = dot(gd, dec_s[...], NN)
    small_ref[5:8, :] = gw[0:3] + gw[3:6]

    heads = head_ones(width, 128, 1)
    for j in range(rows // block):
        gt_s[j * 16 : (j + 1) * 16] = gd[:, j * block : (j + 1) * block]

    @pl.loop(0, rows // block)
    def _(b):
        cut = pl.ds(pl.multiple_of(b * block, block), block)
        g_final = dot(gt_s[pl.ds(pl.multiple_of(b * 16, 16), 16)], w_twice, TN).astype(BF16)
        ga_down[...] += dot(act_s[cut], g_final, TN)
        g_up = (dot(g_final, w_down_ref[...], NT) * gp_s[cut]).astype(BF16)
        ga_up[...] += dot(n2_s[cut], g_up, TN)
        g_normed = dot(g_up, w_up_ref[...], NT)
        xhat, rstd = norm_parts(res_s[cut])
        small_ref[8:9, :] += rowsum(g_normed * xhat)
        g_res = g_final.astype(F32) + norm_back(g_normed, xhat, rstd, gain)
        gres_ref[cut] = g_res
        g_attn = g_res.astype(BF16)
        o = o_s[cut]
        linv = linv_s[cut]
        ga_out[...] += dot(o.astype(BF16), g_attn, TN)
        do = dot(g_attn, w_out_ref[...], NT).astype(BF16)
        do_ref[cut] = do
        dof = do.astype(F32)
        dl_ref[cut] = (dof * linv).astype(BF16)
        ph, pl_ = split2(dof * o)
        cols_ref[cut, 0:HEADS] = ((dot(ph, heads, NN) + dot(pl_, heads, NN)))[:, 0:HEADS]
        for h in range(HEADS):
            cols_ref[cut, HEADS + h : HEADS + h + 1] = linv[:, h * half : h * half + 1]

    gres_copy = pltpu.make_async_copy(gres_ref, gres_out, out_sem.at[0])
    gres_copy.start()
    for g in range(pairs):
        copy(rows // block - 1, g).wait()
    pltpu.make_async_copy(nb_s, nb_ref, nb_sem).wait()

    def write(low_ref, high_ref):
        pieces = [ga_down[...]]
        pieces += [ga_up[:, j * width : (j + 1) * width] for j in range(hidden // width)]
        pieces += [ga_out[...]]
        at = 0
        half = low_ref.shape[0]
        for piece in pieces:
            n = piece.shape[0]
            first = max(0, min(n, half - at))
            if first:
                low_ref[at : at + first, :] = piece[:first].astype(BF16)
            if first < n:
                high_ref[at + first - half : at + n - half, :] = piece[first:].astype(BF16)
            at += n

    @pl.when(me % 2 == 0)
    def _():
        write(keep_ref, send_ref)

    @pl.when(me % 2 == 1)
    def _():
        write(send_ref, keep_ref)

    keep_copy = pltpu.make_async_copy(keep_ref, keep_out, out_sem.at[1])
    keep_copy.start()
    gres_copy.wait()
    keep_copy.wait()


def layer(me, valid_len, library, xa, xb, pb, gain1, w, qa, ka, va, ta, gain, w_out, w_up, w_down, w_dec, gene, tables, block=256):
    part, width = ka.shape
    rows, keys, length = part, 2 * part, part // 2
    hidden = w_up.shape[1]
    pair = 2 * (width // HEADS)
    smem = pl.BlockSpec(memory_space=pltpu.SMEM)
    vmem = pl.BlockSpec(memory_space=pltpu.VMEM)
    half = (2 * hidden + width) // 2
    return call(
        functools.partial(layer_kernel, block=block),
        [
            pltpu.HBM((HEADS, rows, keys), BF16),
            pltpu.HBM((part, width), BF16),
            pltpu.HBM((rows, width), F32),
            pltpu.HBM((half, width), BF16),
            sds((length, width), BF16),
            sds((part, width), BF16),
            sds((part, width), BF16),
            sds((8, width), F32),
            sds((rows, width), BF16),
            sds((rows, width), BF16),
            sds((rows, 128), F32),
            sds((half, width), BF16),
            sds((16, width), F32),
        ],
        flops=24 * rows * width * hidden + 16 * rows * keys * width,
        vmem=40,
        in_specs=[smem] * 3 + [vmem] * 19,
        out_specs=[pl.BlockSpec(memory_space=pltpu.HBM)] * 4 + [vmem] * 9,
        scratch_shapes=[
            pltpu.VMEM((part, width), BF16),
            pltpu.SemaphoreType.DMA,
            pltpu.VMEM((rows, width), F32),
            pltpu.VMEM((half, width), BF16),
            pltpu.SemaphoreType.DMA((2,)),
            pltpu.VMEM((rows, width), BF16),
            pltpu.VMEM((rows, width), BF16),
            pltpu.VMEM((2, 2, block, keys), BF16),
            pltpu.SemaphoreType.DMA((2,)),
            pltpu.VMEM((16 * rows // block, block), BF16),
            pltpu.VMEM((HEADS, keys, pair), BF16),
            pltpu.VMEM((rows, width), F32),
            pltpu.VMEM((rows, width), F32),
            pltpu.VMEM((rows, width), F32),
            pltpu.VMEM((rows, width), BF16),
            pltpu.VMEM((rows, hidden), BF16),
            pltpu.VMEM((rows, hidden), F32),
            pltpu.VMEM((rows, width), BF16),
            pltpu.VMEM((16, rows), F32),
            pltpu.VMEM((16, width), F32),
            pltpu.VMEM((rows // 64, 128), F32),
            pltpu.VMEM((hidden, width), F32),
            pltpu.VMEM((width, hidden), F32),
            pltpu.VMEM((width, width), F32),
        ],
    )(me, valid_len, library, xa, xb, pb, gain1, w, qa, ka, va, ta, gain, w_out, w_up, w_down, w_dec, gene, *tables)


def attend_back_kernel(me_ref, len_ref, qa_ref, qb_ref, do_ref, dl_ref, cols_ref, ka_ref, kb_ref,
                       va_ref, vb_ref, p_ref, dq_ref, dk_ref, dv_ref, ak_ref, av_ref, p_s, p_sem, *, head, block, chunk):
    part, width = ka_ref.shape
    keys = 2 * part
    rows = do_ref.shape[0]
    length = rows // 2
    half = width // HEADS
    pair = 2 * half
    lane = lax.broadcasted_iota(jnp.int32, (1, pair), 1)
    lo = (head % 2) * half
    own = (lane < half) if head % 2 == 0 else (lane >= half)
    at0 = head // 2 * pair
    cols = slice(at0, at0 + pair)
    mine = slice(at0 + lo, at0 + lo + half)

    def copy(b):
        rcut = pl.ds(b * block, block)
        return pltpu.make_async_copy(p_ref.at[head, rcut], p_s.at[rcut], p_sem.at[b])

    for b in range(rows // block):
        copy(b).start()
    for b in range(rows // block):
        cut = slice(b * block, (b + 1) * block)
        at = b * block % length
        q_ref = qa_ref if b * block < length else qb_ref
        q = q_ref[at : at + block, mine]
        do = do_ref[cut, cols]
        do = jnp.where(own, do, jnp.zeros_like(do))
        dl = dl_ref[cut, mine]
        delta = cols_ref[cut, head : head + 1]
        linv = cols_ref[cut, HEADS + head : HEADS + head + 1]
        total = None
        copy(b).wait()
        for c in range(keys // chunk):
            kcut = slice(c * chunk, (c + 1) * chunk)
            k_ref, v_ref = (ka_ref, va_ref) if c * chunk < part else (kb_ref, vb_ref)
            kat = c * chunk % part
            kc = k_ref[kat : kat + chunk, cols]
            dp = dot(do, v_ref[kat : kat + chunk, cols], NT)
            pc = p_s[cut, kcut]
            ds = (pc.astype(F32) * ((dp - delta) * linv)).astype(BF16)
            step = dot(ds, kc, NN)
            total = step if total is None else total + step
            dv = dot(dl, pc, TN)
            dk = dot(q, ds, TN)
            if b == 0:
                av_ref[:, kcut] = dv
                ak_ref[:, kcut] = dk
            else:
                av_ref[:, kcut] += dv
                ak_ref[:, kcut] += dk
        dq_ref[cut] = (jnp.where(own, total, 0.0) * half**-0.5).astype(BF16)
    live = live_keys(me_ref, len_ref, keys)
    dk_ref[...] = jnp.where(live, ak_ref[...], 0.0).astype(BF16)
    dv_ref[...] = jnp.where(live, av_ref[...], 0.0).astype(BF16)


def attend_back(head, me, valid_len, qa, qb, do, dl, cols, ka, kb, va, vb, p, block=512, chunk=512):
    rows = do.shape[0]
    part, width = ka.shape
    keys = 2 * part
    pair = 2 * (width // HEADS)
    smem = pl.BlockSpec(memory_space=pltpu.SMEM)
    vmem = pl.BlockSpec(memory_space=pltpu.VMEM)
    return call(
        functools.partial(attend_back_kernel, head=head, block=block, chunk=chunk),
        [sds((rows, pair), BF16), sds((pair // 2, keys), BF16), sds((pair // 2, keys), BF16)],
        flops=8 * rows * keys * width,
        moved=2 * rows * keys,
        vmem=46,
        in_specs=[smem, smem] + [vmem] * 9 + [pl.BlockSpec(memory_space=pltpu.HBM)],
        out_specs=[vmem] * 3,
        scratch_shapes=[
            pltpu.VMEM((pair // 2, keys), F32),
            pltpu.VMEM((pair // 2, keys), F32),
            pltpu.VMEM((rows, keys), BF16),
            pltpu.SemaphoreType.DMA((rows // block,)),
        ],
    )(me, valid_len, qa, qb, do, dl, cols, ka, kb, va, vb, p)


def weights_kernel(me_ref, na_ref, nb_ref, *refs):
    keep_ref, send_ref = refs[-2:]
    heads = [refs[3 * h : 3 * h + 3] for h in range(HEADS)]
    part, width = na_ref.shape
    length = part // 2
    dim = width // HEADS
    dq = sum(h[0][...].astype(F32) for h in heads[:2]), sum(h[0][...].astype(F32) for h in heads[2:])
    dq = jnp.concatenate(dq, axis=1).astype(BF16)
    gq = dot(na_ref[:length], dq[:length], TN) + dot(nb_ref[:length], dq[length:], TN)
    outs = [gq]
    for j in (1, 2):
        d = jnp.concatenate([h[j][...] for h in heads], axis=0)
        g = dot(d[:, :part], na_ref[...], NN) + dot(d[:, part:], nb_ref[...], NN)
        outs.append(jnp.transpose(g))
    half = 3 * width // 2

    def write(low_ref, high_ref):
        at = 0
        for piece in outs:
            first = max(0, min(width, half - at))
            if first:
                low_ref[at : at + first, :] = piece[:first].astype(BF16)
            if first < width:
                high_ref[at + first - half : at + width - half, :] = piece[first:].astype(BF16)
            at += width

    @pl.when(me_ref[0] % 2 == 0)
    def _():
        write(keep_ref, send_ref)

    @pl.when(me_ref[0] % 2 == 1)
    def _():
        write(send_ref, keep_ref)


def weights(me, na, nb, back):
    part, width = na.shape
    half = 3 * width // 2
    smem = pl.BlockSpec(memory_space=pltpu.SMEM)
    vmem = pl.BlockSpec(memory_space=pltpu.VMEM)
    return call(
        weights_kernel,
        [sds((half, width), BF16)] * 2,
        vmem=16,
        flops=10 * part * width * width,
        moved=16 * part * width,
        in_specs=[smem] + [vmem] * (2 + 3 * HEADS),
        out_specs=[vmem] * 2,
    )(me, na, nb, *[a for b in back for a in b])


def write3(ref, x):
    n = x.shape[0]
    high = x.astype(BF16)
    rest = x - high.astype(F32)
    mid = rest.astype(BF16)
    low = (rest - mid.astype(F32)).astype(BF16)
    ref[0:n] = high
    ref[n : 2 * n] = mid
    ref[2 * n : 3 * n] = low


def read3(x):
    n = x.shape[0] // 3
    return x[:n].astype(F32) + x[n : 2 * n].astype(F32) + x[2 * n :].astype(F32)


def normed_kernel(me_ref, xa_ref, xb_ref, pa_ref, pb_ref, w_ref, small_ref, *refs):
    own_ref, send_ref, three_ref = refs[-3:]
    heads = [refs[3 * h : 3 * h + 3] for h in range(HEADS)]
    length, width = xb_ref.shape
    cell = me_ref[0] // 2
    tt = (((0,), (1,)), ((), ()))
    w = w_ref[...]
    dq = sum(h[0][...].astype(F32) for h in heads[:2]), sum(h[0][...].astype(F32) for h in heads[2:])
    dq = jnp.concatenate(dq, axis=1).astype(BF16)
    dk = jnp.concatenate([h[1][...] for h in heads], axis=0)
    dv = jnp.concatenate([h[2][...] for h in heads], axis=0)
    total = jnp.zeros((1, width), F32)
    for b in range(4):
        cut = slice(b * length, (b + 1) * length)
        gn = dot(dk[:, cut], w[:, width : 2 * width], tt) + dot(dv[:, cut], w[:, 2 * width :], tt)
        at = slice(b // 2 * length, (b // 2 + 1) * length)
        if b % 2 == 0:
            gn += dot(dq[at], w[:, :width], NT)
        x = xa_ref[cell] if b == 0 else (pa_ref, xb_ref, pb_ref)[b - 1][...]
        xhat, _ = norm_parts(x.astype(F32))
        total += jnp.sum(gn * xhat, axis=0, keepdims=True)
        if b % 2 == 0:
            own_ref[at] = gn
        else:
            send_ref[at] = gn.astype(BF16)
    rows = small_ref.shape[0]
    keep = lax.broadcasted_iota(jnp.int32, (rows, 1), 0)
    small = jnp.where(keep < 9, small_ref[...], jnp.where(keep == 9, total, 0.0))
    write3(three_ref, small)


def normed_back(me, xa, xb, pa, pb, w, small, back):
    length, width = xb.shape
    rows = 2 * length
    smem = pl.BlockSpec(memory_space=pltpu.SMEM)
    vmem = pl.BlockSpec(memory_space=pltpu.VMEM)
    return call(
        normed_kernel,
        [sds((rows, width), F32), sds((rows, width), BF16), sds((3 * small.shape[0], width), BF16)],
        vmem=24,
        flops=12 * rows * width * width,
        moved=16 * rows * width,
        in_specs=[smem] + [vmem] * (6 + 3 * HEADS),
        out_specs=[vmem] * 3,
    )(me, xa, xb, pa, pb, w, small, *[a for b in back for a in b])


def tokens_kernel(me_ref, xa_ref, xb_ref, gain_ref, gres_ref, own_ref, got_ref, mine_ref, back_ref):
    length = mine_ref.shape[0]
    for b in range(2):
        cut = slice(b * length, (b + 1) * length)
        x = xa_ref[me_ref[0] // 2] if b == 0 else xb_ref[...]
        xhat, rstd = norm_parts(x.astype(F32))
        gn = own_ref[cut] + got_ref[cut].astype(F32)
        g = gres_ref[cut] + norm_back(gn, xhat, rstd, gain_ref[...])
        if b == 0:
            mine_ref[...] = g
        else:
            back_ref[...] = g.astype(BF16)


def tokens_back(me, xa, xb, gain, gres, own, got):
    length, width = xb.shape
    smem = pl.BlockSpec(memory_space=pltpu.SMEM)
    vmem = pl.BlockSpec(memory_space=pltpu.VMEM)
    return call(
        tokens_kernel,
        [sds((length, width), F32), sds((length, width), BF16)],
        vmem=12,
        flops=60 * length * width,
        moved=24 * length * width,
        in_specs=[smem] + [vmem] * 6,
        out_specs=[vmem] * 2,
    )(me, xa, xb, gain, gres, own, got)


def join_kernel(a_ref, b_ref, three_ref, o_ref):
    n = a_ref.shape[0]
    o_ref[:n] = (a_ref[...].astype(F32) + b_ref[...].astype(F32)).astype(BF16)
    o_ref[n:] = three_ref[...]


def merge_kernel(a_ref, b_ref, o_ref, *, small):
    n = a_ref.shape[0] - small
    o_ref[:n] = (a_ref[:n].astype(F32) + b_ref[:n].astype(F32)).astype(BF16)
    write3(o_ref.at[n:], read3(a_ref[n:]) + read3(b_ref[n:]))


def join(a, b, three):
    vmem = pl.BlockSpec(memory_space=pltpu.VMEM)
    shape = (a.shape[0] + three.shape[0], a.shape[1])
    return call(join_kernel, sds(shape, BF16), moved=6 * a.size, vmem=4, in_specs=[vmem] * 3, out_specs=vmem)(a, b, three)


def merge(a, b, small):
    vmem = pl.BlockSpec(memory_space=pltpu.VMEM)
    kernel = functools.partial(merge_kernel, small=small)
    return call(kernel, sds(a.shape, BF16), moved=6 * a.size, vmem=4, in_specs=[vmem] * 2, out_specs=vmem)(a, b)


def unpack_main_kernel(me_ref, own_ref, got_ref, down_ref, up_ref, out_ref):
    hidden, width = down_ref.shape

    def write(low_ref, high_ref):
        half = low_ref.shape[0]

        def rows(start, stop):
            if stop <= half:
                return low_ref[start:stop].astype(F32)
            return high_ref[start - half : stop - half].astype(F32)

        step = math.gcd(half, width)
        for at in range(0, hidden, step):
            down_ref[at : at + step] = rows(at, at + step)
        for j in range(hidden // width):
            for at in range(0, width, step):
                start = hidden + j * width + at
                up_ref[at : at + step, j * width : (j + 1) * width] = rows(start, start + step)
        for at in range(0, width, step):
            out_ref[at : at + step] = rows(2 * hidden + at, 2 * hidden + at + step)

    @pl.when(me_ref[0] % 2 == 0)
    def _():
        write(own_ref, got_ref)

    @pl.when(me_ref[0] % 2 == 1)
    def _():
        write(got_ref, own_ref)


def unpack_main(me, own, got, hidden):
    width = own.shape[1]
    smem = pl.BlockSpec(memory_space=pltpu.SMEM)
    vmem = pl.BlockSpec(memory_space=pltpu.VMEM)
    return call(
        unpack_main_kernel,
        [sds((hidden, width), F32), sds((width, hidden), F32), sds((width, width), F32)],
        vmem=12,
        moved=12 * hidden * width,
        in_specs=[smem, vmem, vmem],
        out_specs=[vmem] * 3,
    )(me, own, got)


def finish_kernel(me_ref, own_ref, got_ref, qkv_ref, gain1_ref, gain2_ref, dec_ref, sum_ref):
    width = gain1_ref.shape[1]
    half = 3 * width // 2

    def write(low_ref, high_ref):
        step = math.gcd(half, width)
        for j in range(3):
            for at in range(0, width, step):
                start = j * width + at
                ref, first = (low_ref, start) if start < half else (high_ref, start - half)
                qkv_ref[at : at + step, j * width : (j + 1) * width] = ref[first : first + step].astype(F32)

    @pl.when(me_ref[0] % 2 == 0)
    def _():
        write(own_ref, got_ref)

    @pl.when(me_ref[0] % 2 == 1)
    def _():
        write(got_ref, own_ref)

    small = read3(own_ref[half:]) + read3(got_ref[half:])
    gain1_ref[...] = small[9:10]
    gain2_ref[...] = small[8:9]
    dec_ref[...] = small[5:8]
    sums = jnp.sum(small, axis=1, keepdims=True)
    count = sums[4:5]
    rms = jnp.sqrt(sums[0:3] / (count * width))
    lane = lax.broadcasted_iota(jnp.int32, (1, 4), 1)
    out = jnp.where(lane == 0, sums[3:4] / count, 0.0)
    for j in range(3):
        out = jnp.where(lane == j + 1, rms[j : j + 1], out)
    sum_ref[...] = out


def finish(me, own, got):
    width = own.shape[1]
    smem = pl.BlockSpec(memory_space=pltpu.SMEM)
    vmem = pl.BlockSpec(memory_space=pltpu.VMEM)
    return call(
        finish_kernel,
        [sds((width, 3 * width), F32), sds((1, width), F32), sds((1, width), F32), sds((3, width), F32), sds((1, 4), F32)],
        vmem=8,
        moved=12 * 3 * width * width,
        in_specs=[smem] + [vmem] * 2,
        out_specs=[vmem] * 5,
    )(me, own, got)


AXES = ("cells", "slots")


def devices():
    return lax.axis_size("cells") * lax.axis_size("slots")


def swap(x, mask, odd=None):
    odd = mask if odd is None else odd
    return lax.ppermute(x, AXES, [(i, i ^ (odd if i % 2 else mask)) for i in range(devices())])


def routes():
    slots = lax.axis_size("slots")
    near, far = [slots, 2 * slots], []
    bit = 4 * slots
    while bit < devices():
        far.append(bit)
        bit *= 2
    return list(zip(near + far + [2], near[::-1] + [2] + far))


def after(x, *others):
    return lax.optimization_barrier((x, *others))[0]


def per_device(
    tokens,
    valid_len,
    library,
    gene_slot,
    counts,
    norm1_gain,
    w_qkv,
    w_out,
    norm2_gain,
    w_up,
    w_down,
    w_decoder,
):
    cells, length, width = tokens.shape
    hidden = w_up.shape[1]
    slot = lax.axis_index("slots")
    cell = slot // 2
    me = jnp.full((1,), slot, jnp.int32)
    pick = lambda a: lax.dynamic_index_in_dim(a, cell, 0, keepdims=False)
    other = lambda a: lax.dynamic_index_in_dim(a, 1 - cell, 0, keepdims=False)

    came = swap(other(tokens), 2)
    near = swap(pick(tokens), 1)
    mine_counts = pick(counts)[None]
    away_counts = other(counts)[None]
    tables = (mine_counts, swap(mine_counts, 1), swap(away_counts, 2), swap(away_counts, 3))
    gain1 = norm1_gain[None]
    gain2 = norm2_gain[None]

    na, qa, ka, va, ta = qkv(me, valid_len, tokens, near, gain1, w_qkv, 0)
    came = after(came, ta)
    far = swap(came, 1)
    p, nb, gres, keep, qb, kb, vb, _, do, dl, cols, send, small = layer(
        me, valid_len, library, tokens, came, far, gain1, w_qkv, qa, ka, va, ta,
        gain2, w_out, w_up, w_down, w_decoder, gene_slot, tables,
    )

    order = routes()
    number = lax.axis_index("cells") * lax.axis_size("slots") + slot
    sides = [jnp.where(slot % 2 == 0, number // even, number // odd) % 2 for even, odd in order[:2]]

    def halve(x, side):
        n = x.shape[0] // 2
        return lax.dynamic_slice_in_dim(x, side * n, n, 0), lax.dynamic_slice_in_dim(x, (1 - side) * n, n, 0)

    def whole(own, got, side):
        return jnp.where(side == 0, jnp.concatenate([own, got], 0), jnp.concatenate([got, own], 0))

    def back(h, p):
        return attend_back(h, me, valid_len, qa, qb, do, dl, cols, ka, kb, va, vb, p)

    got = swap(send, 1)
    backs = [back(0, p)]
    main = keep + after(got, backs[0][0])
    for i in range(2):
        mine, away = halve(main, sides[i])
        got = swap(away, *order[i])
        backs.append(back(1 + i, after(p, away)))
        main = mine + after(got, backs[-1][0])
    got = swap(main, *order[2])
    backs.append(back(3, after(p, main)))
    main = main + after(got, backs[-1][0])
    got = swap(main, *order[3])

    keep, send = weights(me, na, nb, backs)
    final_got = swap(send, 1)
    gn_own, gn_send, three = normed_back(me, tokens, came, near, far, w_qkv, small, backs)
    rows3 = three.shape[0]
    gn_got = swap(gn_send, 1)
    final = join(keep, final_got, three)
    final_got = swap(final, *order[0])
    main = main + after(got, final)
    for masks in order[4:]:
        main = main + swap(main, *masks)
    got = swap(main, *order[1])
    mine, away = tokens_back(me, tokens, came, gain1, gres, gn_own, gn_got)
    returned = swap(away, 2)
    final = merge(final, final_got, rows3)
    final_got = swap(final, *order[1])
    main = whole(main, after(got, final), sides[1])
    got = swap(main, *order[0])
    final = merge(final, final_got, rows3)
    final_got = swap(final, *order[2])
    main = whole(main, after(got, final), sides[0])
    got = swap(main, 1)
    final = merge(final, final_got, rows3)
    for masks in order[3:]:
        final_got = swap(final, *masks)
        final = merge(final, final_got, rows3)
    g_down, g_up, g_out = unpack_main(me, main, got, hidden)
    returned = returned.astype(F32)
    grad_tokens = jnp.where(cell == 0, jnp.stack([mine, returned]), jnp.stack([returned, mine]))
    g_qkv, g_gain1, g_gain2, g_dec, summary = finish(me, final, swap(final, 1))
    return (grad_tokens, g_gain1[0], g_qkv, g_out, g_gain2[0], g_up, g_down, g_dec, summary[0])


def solution(mesh):
    in_specs = (
        P("cells", "slots", None),
        P("cells"),
        P("cells"),
        P("cells", None),
        P("cells", "slots"),
        P(),
        P(),
        P(),
        P(),
        P(),
        P(),
        P(),
    )
    out_specs = (P("cells", "slots", None), P(), P(), P(), P(), P(), P(), P(), P())
    return jax.shard_map(
        per_device, mesh=mesh, in_specs=in_specs, out_specs=out_specs, check_vma=False
    )
```

time: 163 us -> 124 us (0.76)
  waiting for transfers between devices: 49.8 us -> 17.8 us
  starting transfers between devices: 15.3 us -> 22.8 us
  between operations: 5.82 us -> 1.2 us
  Pallas kernels: 70.6 us -> 67.1 us
  local copies, waits for them, and re-layouts: 11.2 us -> 8.29 us
  other arithmetic: 9.25 us -> 6.52 us
    ppermute x13 -> x22, waiting for transfers between devices: 49.8 us -> 17.8 us  [swap(): lax.ppermute(x, AXES, [(i, i ^ (odd if i % 2 else mask)) for i in range(d...]
    ppermute x13 -> x22, starting transfers between devices: 15.3 us -> 22.8 us  [swap(): lax.ppermute(x, AXES, [(i, i ^ (odd if i % 2 else mask)) for i in range(d...]
    unnamed x27 -> x68, local copies, waits for them, and re-layouts: 1.7 us -> 7.08 us
    concatenate x9 -> x0, other arithmetic: 4.47 us -> none  [the longest x2 2.02 us: per_device(): jnp.concatenate(list(a.reshape(-1, width, width)), axis=1)]
    slice x6 -> x0, local copies, waits for them, and re-layouts: 3.57 us -> none  [the longest x1 1.04 us: per_device(): parts.append(main[at:at + size])]
    pallas_call x7 -> x16, Pallas kernels: 70.6 us -> 67.1 us  [the longest x1 29.7 us: layer(): call(functools.partial(layer_kernel, block=block), [pltpu.HBM((HEADS, row...]
    select_n x1 -> x2, other arithmetic: 0.3 us -> 3.34 us  [whole(): jnp.where(side == 0, jnp.concatenate([own, got], 0), jnp.concatenate([got...]
    dynamic_slice x6 -> x3, local copies, waits for them, and re-layouts: 1.96 us -> 0.06 us  [the longest x2 0.05 us: halve(): lax.dynamic_slice_in_dim(x, (1 - side) * n, n, 0)]
  transfers between devices with their start and end apart: 13 -> 22, of which waited for: 7 -> 11; matrix products, arithmetic and copies ran while one was open for 6% -> 4% of each run, Pallas kernels for 2% -> 29%
where the time goes in v2:
time: 124 us
  Pallas kernels  67.1 us (54%)
  starting transfers between devices  22.8 us (18%)
  waiting for transfers between devices  17.8 us (14%)
  local copies, waits for them, and re-layouts  8.29 us (7%)
  other arithmetic  6.52 us (5%)
    pallas_call x1, Pallas kernels, layer(): call(functools.partial(layer_kernel, block=block), [pltpu.HBM((HEADS, row...  29.7 us
    pallas_call x4, Pallas kernels, attend_back(): call(functools.partial(attend_back_kernel, head=head, block=block, chunk=...  26.9 us
    ppermute x22, starting transfers between devices, swap(): lax.ppermute(x, AXES, [(i, i ^ (odd if i % 2 else mask)) for i in range(d...  22.8 us
    ppermute x22, waiting for transfers between devices, swap(): lax.ppermute(x, AXES, [(i, i ^ (odd if i % 2 else mask)) for i in range(d...  17.8 us
    unnamed x68, local copies, waits for them, and re-layouts  7.08 us
    select_n x2, other arithmetic, whole(): jnp.where(side == 0, jnp.concatenate([own, got], 0), jnp.concatenate([got...  3.34 us
    pallas_call x1, Pallas kernels, tokens_back(): call(tokens_kernel, [sds((length, width), F32), sds((length, width), BF16...  2.49 us
  transfers between devices with their start and end apart: 22, of which 11 were waited for; matrix products, arithmetic and copies ran while one was open for 4% of the time, Pallas kernels for 29%

profile of v2, /device:TPU:0, one launch (start us, length us, event | category | flops | bytes accessed | tf_op | source)
XLA Modules:
  0.0 123.8 jit_solution(10796448156214136170)
XLA Ops:
  0.8 1.1 dynamic-slice_bitcast_fusion
  2.4 2.6 %collective-permute-start = (bf16[512,256]{1,0:T(8,128)(2,1)S(1)}, bf16[512,256]{1,0:T(8,128)(2,1)S(1)}, u32[]{:S(2)}, u32[]{:S(2)}) collective-permute-start(bf16[512,256]{1,0:T(8,128)(2,1)S(1)} %get-tuple-element.120), channel_id=1, source_target_pairs={{0,2},{1,3},{2,0},{3,1},{4,6},{5,7},{6,4},{7,5},{8,10},{9,11},{10,... | collective-permute-start | bytes 786440 | tf_op jit(solution)/shard_map/ppermute | solution.py:832
  5.0 1.1 copy-done.2
  8.5 2.2 %shard_map.187 = (bf16[1024,256]{1,0:T(8,128)(2,1)}, bf16[512,256]{1,0:T(8,128)(2,1)S(1)}, bf16[1024,256]{1,0:T(8,128)(2,1)S(1)}, bf16[1024,256]{1,0:T(8,128)(2,1)S(1)}, f32[8,256]{1,0:T(8,128)S(1)}) custom-call(s32[1]{0:T(128)} %bitcast.me_ref, s32[2]{0:T(128)S(1)} %copy-done.21, bf16[2,512,256]{2,1,0:T(8,128)(2,1)S(1)} %copy-done.2, ...), custom_call_target="tpu_custom_call" | custom-call | flops 402653184 | bytes 2621440 | tf_op jit(solution)/shard_map/pallas_call | solution.py:115
  10.7 1.2 %collective-permute-done.xb_ref = bf16[512,256]{1,0:T(8,128)(2,1)S(1)} collective-permute-done((bf16[512,256]{1,0:T(8,128)(2,1)S(1)}, bf16[512,256]{1,0:T(8,128)(2,1)S(1)}, u32[]{:S(2)}, u32[]{:S(2)}) %collective-permute-start) | collective-permute-done | bytes 262176 | tf_op jit(solution)/shard_map/ppermute | solution.py:832
  12.0 1.9 %collective-permute-start.5 = (s32[1,512]{1,0:T(1,128)S(1)}, s32[1,512]{1,0:T(1,128)S(1)}, u32[]{:S(2)}, u32[]{:S(2)}) collective-permute-start(s32[1,512]{1,0:T(1,128)S(1)} %get-tuple-element.121), channel_id=1, source_target_pairs={{0,3},{1,2},{2,1},{3,0},{4,7},{5,6},{6,5},{7,4},{8,11},{9,10},{10,... | collective-permute-start | bytes 6152 | tf_op jit(solution)/shard_map/ppermute | solution.py:832
  14.2 1.0 collective-permute-done.5.c3_ref
  15.2 2.3 %collective-permute-done.4.c2_ref = s32[1,512]{1,0:T(1,128)S(1)} collective-permute-done((s32[1,512]{1,0:T(1,128)S(1)}, s32[1,512]{1,0:T(1,128)S(1)}, u32[]{:S(2)}, u32[]{:S(2)}) %collective-permute-start.4) | collective-permute-done | bytes 2080 | tf_op jit(solution)/shard_map/ppermute | solution.py:832
  17.6 29.7 %shard_map.188 = (bf16[4,1024,2048]{2,1,0:T(8,128)(2,1)}, bf16[1024,256]{1,0:T(8,128)(2,1)}, f32[1024,256]{1,0:T(8,128)}, bf16[1152,256]{1,0:T(8,128)(2,1)}, bf1...) custom-call(s32[1]{0:T(128)} %bitcast.me_ref, ...), custom_call_target="tpu_custom_call" | custom-call | flops 15032385536 | tf_op jit(solution)/shard_map/pallas_call | solution.py:433
  48.9 1.0 copy-done.1
  50.9 6.5 %shard_map.189 = (bf16[1024,128]{1,0:T(8,128)(2,1)S(1)}, bf16[64,2048]{1,0:T(8,128)(2,1)S(1)}, bf16[64,2048]{1,0:T(8,128)(2,1)S(1)}) custom-call(s32[1]{0:T(128)} %bitcast.me_ref, s32[2]{0:T(128)S(1)} %copy-done.22, bf16[512,256]{1,0:T(8,128)(2,1)S(1)} %get-tuple-element.66.qa_ref, bf16[512,256]{1,0:T(8,128)(2,1)S(1)} %copy-done.6, ...), custom_call_target="tpu_custom_call" | custom-call | flops 4294967296 | bytes 4194304 | tf_op jit(solution)/shard_map/pallas_call | solution.py:547
  57.4 1.2 add.57
  58.6 1.6 %collective-permute-start.7 = (bf16[576,256]{1,0:T(8,128)(2,1)S(1)}, bf16[576,256]{1,0:T(8,128)(2,1)S(1)}, u32[]{:S(2)}, u32[]{:S(2)}) collective-permute-start(bf16[576,256]{1,0:T(8,128)(2,1)S(1)} %constant_dynamic-slice_fusion.1), channel_id=1, source_target_pairs={{0,4},{1,9},{2,6},{3,11},{4,0},{5,13},{6,2},{7,15},{8,12},{9,1},{1... | collective-permute-start | bytes 884744 | tf_op jit(solution)/shard_map/ppermute | solution.py:832
  60.2 6.8 %shard_map.190 = (bf16[1024,128]{1,0:T(8,128)(2,1)S(1)}, bf16[64,2048]{1,0:T(8,128)(2,1)S(1)}, bf16[64,2048]{1,0:T(8,128)(2,1)S(1)}) custom-call(s32[1]{0:T(128)} %bitcast.me_ref, s32[2]{0:T(128)S(1)} %copy-done.22, bf16[512,256]{1,0:T(8,128)(2,1)S(1)} %get-tuple-element.66.qa_ref, bf16[512,256]{1,0:T(8,128)(2,1)S(1)} %copy-done.6, ...), custom_call_target="tpu_custom_call" | custom-call | flops 4294967296 | bytes 4194304 | tf_op jit(solution)/shard_map/pallas_call | solution.py:547
  67.2 1.6 %collective-permute-start.8 = (bf16[288,256]{1,0:T(8,128)(2,1)S(1)}, bf16[288,256]{1,0:T(8,128)(2,1)S(1)}, u32[]{:S(2)}, u32[]{:S(2)}) collective-permute-start(bf16[288,256]{1,0:T(8,128)(2,1)S(1)} %constant_dynamic-slice_fusion), channel_id=1, source_target_pairs={{0,8},{1,5},{2,10},{3,7},{4,12},{5,1},{6,14},{7,3},{8,0},{9,13},{1... | collective-permute-start | bytes 442376 | tf_op jit(solution)/shard_map/ppermute | solution.py:832
  68.8 6.7 %shard_map.191 = (bf16[1024,128]{1,0:T(8,128)(2,1)S(1)}, bf16[64,2048]{1,0:T(8,128)(2,1)S(1)}, bf16[64,2048]{1,0:T(8,128)(2,1)S(1)}) custom-call(s32[1]{0:T(128)} %bitcast.me_ref, s32[2]{0:T(128)S(1)} %copy-done.22, bf16[512,256]{1,0:T(8,128)(2,1)S(1)} %get-tuple-element.66.qa_ref, bf16[512,256]{1,0:T(8,128)(2,1)S(1)} %copy-done.6, ...), custom_call_target="tpu_custom_call" | custom-call | flops 4294967296 | bytes 4194304 | tf_op jit(solution)/shard_map/pallas_call | solution.py:547
  75.6 2.6 %collective-permute-start.17 = (bf16[288,256]{1,0:T(8,128)(2,1)S(1)}, bf16[288,256]{1,0:T(8,128)(2,1)S(1)}, u32[]{:S(2)}, u32[]{:S(2)}) collective-permute-start(bf16[288,256]{1,0:T(8,128)(2,1)S(1)} %dynamic-slice_add_fusion.1), channel_id=1, source_target_pairs={{0,16},{1,3},{2,18},{3,1},{4,20},{5,7},{6,22},{7,5},{8,24},{9,11},... | collective-permute-start | bytes 442376 | tf_op jit(solution)/shard_map/ppermute | solution.py:832
  78.3 6.8 %shard_map.192 = (bf16[1024,128]{1,0:T(8,128)(2,1)S(1)}, bf16[64,2048]{1,0:T(8,128)(2,1)S(1)}, bf16[64,2048]{1,0:T(8,128)(2,1)S(1)}) custom-call(s32[1]{0:T(128)} %bitcast.me_ref, s32[2]{0:T(128)S(1)} %copy-done.22, bf16[512,256]{1,0:T(8,128)(2,1)S(1)} %get-tuple-element.66.qa_ref, bf16[512,256]{1,0:T(8,128)(2,1)S(1)} %copy-done.6, ...), custom_call_target="tpu_custom_call" | custom-call | flops 4294967296 | bytes 4194304 | tf_op jit(solution)/shard_map/pallas_call | solution.py:547
  87.0 2.0 %shard_map.193 = (f32[1024,256]{1,0:T(8,128)S(1)}, bf16[1024,256]{1,0:T(8,128)(2,1)}, bf16[48,256]{1,0:T(8,128)(2,1)S(1)}) custom-call(s32[1]{0:T(128)} %bitcast.me_ref, bf16[2,512,256]{2,1,0:T(8,128)(2,1)S(1)} %copy-done.4, bf16[512,256]{1,0:T(8,128)(2,1)S(1)} %copy-done.9, bf16[512,256]{1,0:T(8,128)(2,1)S(1)} %copy-done.18, ...), custom_call_target="tpu_custom_call" | custom-call | flops 805306368 | bytes 4194304 | tf_op jit(solution)/shard_map/pallas_call | solution.py:667
  89.7 1.9 %collective-permute-done.18 = bf16[288,256]{1,0:T(8,128)(2,1)S(1)} collective-permute-done((bf16[288,256]{1,0:T(8,128)(2,1)S(1)}, bf16[288,256]{1,0:T(8,128)(2,1)S(1)}, u32[]{:S(2)}, u32[]{:S(2)}) %collective-permute-start.18) | collective-permute-done | bytes 147488 | tf_op jit(solution)/shard_map/ppermute | solution.py:832
  92.8 1.6 %collective-permute-start.9 = (bf16[1024,256]{1,0:T(8,128)(2,1)}, bf16[1024,256]{1,0:T(8,128)(2,1)}, u32[]{:S(2)}, u32[]{:S(2)}) collective-permute-start(bf16[1024,256]{1,0:T(8,128)(2,1)} %get-tuple-element.99), channel_id=1, source_target_pairs={{0,1},{1,0},{2,3},{3,2},{4,5},{5,4},{6,7},{7,6},{8,9},{9,8},{10,11... | collective-permute-start | bytes 1572872 | tf_op jit(solution)/shard_map/ppermute | solution.py:832
  95.7 2.1 %collective-permute-done.19 = bf16[288,256]{1,0:T(8,128)(2,1)} collective-permute-done((bf16[288,256]{1,0:T(8,128)(2,1)}, bf16[288,256]{1,0:T(8,128)(2,1)}, u32[]{:S(2)}, u32[]{:S(2)}) %collective-permute-start.19) | collective-permute-done | bytes 147488 | tf_op jit(solution)/shard_map/ppermute | solution.py:832
  97.8 1.9 %maximum_select_fusion.2 = bf16[576,256]{1,0:T(8,128)(2,1)} fusion(bf16[288,256]{1,0:T(8,128)(2,1)} %collective-permute-done.19, bf16[288,256]{1,0:T(8,128)(2,1)} %add.69, pred[]{:T(512)S(6)} %eq.21), kind=kLoop, calls=%fused_computation.2 | loop fusion | flops 1327104 | bytes 589825 | tf_op jit(solution)/shard_map/jit(_where)/select_n | solution.py:896
  101.2 1.3 %collective-permute-start.14 = (bf16[432,256]{1,0:T(8,128)(2,1)S(1)}, bf16[432,256]{1,0:T(8,128)(2,1)S(1)}, u32[]{:S(2)}, u32[]{:S(2)}) collective-permute-start(bf16[432,256]{1,0:T(8,128)(2,1)S(1)} %shard_map.198.a_ref), channel_id=1, source_target_pairs={{0,16},{1,3},{2,18},{3,1},{4,20},{5,7},{6,22},{7,5},{8,24},{9,11},... | collective-permute-start | bytes 663560 | tf_op jit(solution)/shard_map/ppermute | solution.py:832
  102.5 2.5 %shard_map.194 = (f32[512,256]{1,0:T(8,128)S(1)}, bf16[512,256]{1,0:T(8,128)(2,1)}) custom-call(s32[1]{0:T(128)} %bitcast.me_ref, bf16[2,512,256]{2,1,0:T(8,128)(2,1)S(1)} %copy-done.4, bf16[512,256]{1,0:T(8,128)(2,1)S(1)} %copy-done.9, f32[1,256]{1,0:T(1,128)S(1)} %bitcast.17, f32[1024,256]{1,0:T(8,128)S(1)} %copy-done.7, ...), custom_call_target="tpu_custom_call" | custom-call | flops 7864320 | bytes 3145728 | tf_op jit(solution)/shard_map/pallas_call | solution.py:696
  105.6 1.1 collective-permute-done.20
  106.7 3.8 %collective-permute-done.14.b_ref = bf16[432,256]{1,0:T(8,128)(2,1)S(1)} collective-permute-done((bf16[432,256]{1,0:T(8,128)(2,1)S(1)}, bf16[432,256]{1,0:T(8,128)(2,1)S(1)}, u32[]{:S(2)}, u32[]{:S(2)}) %collective-permute-start.14) | collective-permute-done | bytes 221216 | tf_op jit(solution)/shard_map/ppermute | solution.py:832
  110.5 5.2 %collective-permute-start.15 = (bf16[432,256]{1,0:T(8,128)(2,1)S(1)}, bf16[432,256]{1,0:T(8,128)(2,1)S(1)}, u32[]{:S(2)}, u32[]{:S(2)}) collective-permute-start(bf16[432,256]{1,0:T(8,128)(2,1)S(1)} %shard_map.199.a_ref), channel_id=1, source_target_pairs={{0,2},{1,17},{2,0},{3,19},{4,6},{5,21},{6,4},{7,23},{8,10},{9,25},... | collective-permute-start | bytes 663560 | tf_op jit(solution)/shard_map/ppermute | solution.py:832
  115.8 1.4 %maximum_select_fusion.1.own_ref = bf16[1152,256]{1,0:T(8,128)(2,1)S(1)} fusion(bf16[576,256]{1,0:T(8,128)(2,1)} %collective-permute-done.20, bf16[576,256]{1,0:T(8,128)(2,1)} %maximum_select_fusion.2, pred[]{:T(512)S(6)} %eq.20), kind=kLoop, calls=%fused_computation.1 | loop fusion | flops 2654208 | bytes 1179649 | tf_op jit(solution)/shard_map/jit(_where)/select_n | solution.py:896
  117.3 2.4 %collective-permute-done.15.b_ref = bf16[432,256]{1,0:T(8,128)(2,1)S(1)} collective-permute-done((bf16[432,256]{1,0:T(8,128)(2,1)S(1)}, bf16[432,256]{1,0:T(8,128)(2,1)S(1)}, u32[]{:S(2)}, u32[]{:S(2)}) %collective-permute-start.15) | collective-permute-done | bytes 221216 | tf_op jit(solution)/shard_map/ppermute | solution.py:832
  119.9 1.0 maximum_select_fusion
  122.2 1.6 %shard_map.202 = (f32[1024,256]{1,0:T(8,128)}, f32[256,1024]{1,0:T(8,128)}, f32[256,256]{1,0:T(8,128)}) custom-call(s32[1]{0:T(128)} %bitcast.me_ref, bf16[1152,256]{1,0:T(8,128)(2,1)S(1)} %maximum_select_fusion.1.own_ref, bf16[1152,256]{1,0:T(8,128)(2,1)S(1)} %collective-permute-done.21.got_ref), custom_call_target="tpu_custom_call" | custom-call | bytes 3145728 | tf_op jit(solution)/shard_map/pallas_call | solution.py:765
  (109 shorter events, 14.5 us)
Async XLA Ops:
  0.7 16.8 %copy-start.30 = (f32[256]{0:T(256)S(1)}, f32[256]{0:T(256)}, u32[]{:S(2)}) copy-start(f32[256]{0:T(256)} %param.20) | copy-start | bytes 3076
  0.7 16.8 %copy-start.29 = (bf16[3,256]{1,0:T(4,128)(2,1)S(1)}, bf16[3,256]{1,0:T(4,128)(2,1)}, u32[]{:S(2)}) copy-start(bf16[3,256]{1,0:T(4,128)(2,1)} %w_dec_ref.1) | copy-start | bytes 4612
  0.7 16.8 %copy-start.28 = (s32[2,2048]{1,0:T(2,128)S(1)}, s32[2,2048]{1,0:T(2,128)}, u32[]{:S(2)}) copy-start(s32[2,2048]{1,0:T(2,128)} %gene_ref.1) | copy-start | bytes 49156
  0.7 16.8 %copy-start.3 = (bf16[2,512,256]{2,1,0:T(8,128)(2,1)S(1)}, bf16[2,512,256]{2,1,0:T(8,128)(2,1)}, u32[]{:S(2)}) copy-start(bf16[2,512,256]{2,1,0:T(8,128)(2,1)} %xa_ref.5) | copy-start | bytes 1572868
  0.7 16.8 %copy-start.15 = (bf16[256,768]{1,0:T(8,128)(2,1)S(1)}, bf16[256,768]{1,0:T(8,128)(2,1)}, u32[]{:S(2)}) copy-start(bf16[256,768]{1,0:T(8,128)(2,1)} %w_ref.5) | copy-start | bytes 1179652
  0.7 16.8 %copy-start.22 = (s32[2]{0:T(128)S(1)}, s32[2]{0:T(128)}, u32[]{:S(2)}) copy-start(s32[2]{0:T(128)} %len_ref.11) | copy-start | bytes 28
  0.7 16.8 %copy-start.24 = (f32[256]{0:T(256)S(1)}, f32[256]{0:T(256)}, u32[]{:S(2)}) copy-start(f32[256]{0:T(256)} %param.17) | copy-start | bytes 3076
  0.8 16.8 %copy-start.27 = (bf16[256,256]{1,0:T(8,128)(2,1)S(1)}, bf16[256,256]{1,0:T(8,128)(2,1)}, u32[]{:S(2)}) copy-start(bf16[256,256]{1,0:T(8,128)(2,1)} %w_out_ref.1) | copy-start | bytes 393220
  1.9 3.1 %collective-permute-start.1 = (bf16[512,256]{1,0:T(8,128)(2,1)S(1)}, bf16[512,256]{1,0:T(8,128)(2,1)S(1)}, u32[]{:S(2)}, u32[]{:S(2)}) collective-permute-start(bf16[512,256]{1,0:T(8,128)(2,1)S(1)} %get-tuple-element.119), channel_id=1, source_target_pairs={{0,1},{1,0},{2,3},{3,2},{4,5},{5,4},{6,7},{7,6},{8,9},{9,8},{10,11... | collective-permute-start | bytes 786440 | tf_op jit(solution)/shard_map/ppermute | solution.py:832
  2.4 9.5 %collective-permute-start = (bf16[512,256]{1,0:T(8,128)(2,1)S(1)}, bf16[512,256]{1,0:T(8,128)(2,1)S(1)}, u32[]{:S(2)}, u32[]{:S(2)}) collective-permute-start(bf16[512,256]{1,0:T(8,128)(2,1)S(1)} %get-tuple-element.120), channel_id=1, source_target_pairs={{0,2},{1,3},{2,0},{3,1},{4,6},{5,7},{6,4},{7,5},{8,10},{9,11},{10,... | collective-permute-start | bytes 786440 | tf_op jit(solution)/shard_map/ppermute | solution.py:832
  11.9 35.4 %copy-start.8 = (bf16[512,256]{1,0:T(8,128)(2,1)}, bf16[512,256]{1,0:T(8,128)(2,1)S(1)}, u32[]{:S(2)}) copy-start(bf16[512,256]{1,0:T(8,128)(2,1)S(1)} %collective-permute-done.xb_ref) | copy-start | bytes 786436
  11.9 5.5 %collective-permute-start.2 = (bf16[512,256]{1,0:T(8,128)(2,1)S(1)}, bf16[512,256]{1,0:T(8,128)(2,1)S(1)}, u32[]{:S(2)}, u32[]{:S(2)}) collective-permute-start(bf16[512,256]{1,0:T(8,128)(2,1)S(1)} %collective-permute-done.xb_ref), channel_id=1, source_target_pairs={{0,1},{1,0},{2,3},{3,2},{4,5},{5,4},{6,7},{7,6},{8,9},{9,8},{10,11... | collective-permute-start | bytes 786440 | tf_op jit(solution)/shard_map/ppermute | solution.py:832
  12.0 3.2 %collective-permute-start.5 = (s32[1,512]{1,0:T(1,128)S(1)}, s32[1,512]{1,0:T(1,128)S(1)}, u32[]{:S(2)}, u32[]{:S(2)}) collective-permute-start(s32[1,512]{1,0:T(1,128)S(1)} %get-tuple-element.121), channel_id=1, source_target_pairs={{0,3},{1,2},{2,1},{3,0},{4,7},{5,6},{6,5},{7,4},{8,11},{9,10},{10,... | collective-permute-start | bytes 6152 | tf_op jit(solution)/shard_map/ppermute | solution.py:832
  13.9 3.6 %collective-permute-start.4 = (s32[1,512]{1,0:T(1,128)S(1)}, s32[1,512]{1,0:T(1,128)S(1)}, u32[]{:S(2)}, u32[]{:S(2)}) collective-permute-start(s32[1,512]{1,0:T(1,128)S(1)} %get-tuple-element.121), channel_id=1, source_target_pairs={{0,2},{1,3},{2,0},{3,1},{4,6},{5,7},{6,4},{7,5},{8,10},{9,11},{10,... | collective-permute-start | bytes 6152 | tf_op jit(solution)/shard_map/ppermute | solution.py:832
  14.2 3.3 %collective-permute-start.3 = (s32[1,512]{1,0:T(1,128)S(1)}, s32[1,512]{1,0:T(1,128)S(1)}, u32[]{:S(2)}, u32[]{:S(2)}) collective-permute-start(s32[1,512]{1,0:T(1,128)S(1)} %get-tuple-element.122.c0_ref), channel_id=1, source_target_pairs={{0,1},{1,0},{2,3},{3,2},{4,5},{5,4},{6,7},{7,6},{8,9},{9,8},{10,11... | collective-permute-start | bytes 6152 | tf_op jit(solution)/shard_map/ppermute | solution.py:832
  17.5 29.9 %copy-start.19 = (bf16[512,256]{1,0:T(8,128)(2,1)}, bf16[512,256]{1,0:T(8,128)(2,1)S(1)}, u32[]{:S(2)}) copy-start(bf16[512,256]{1,0:T(8,128)(2,1)S(1)} %collective-permute-done.2.pb_ref) | copy-start | bytes 786436
  48.9 8.5 %collective-permute-start.6 = (bf16[1152,256]{1,0:T(8,128)(2,1)}, bf16[1152,256]{1,0:T(8,128)(2,1)}, u32[]{:S(2)}, u32[]{:S(2)}) collective-permute-start(bf16[1152,256]{1,0:T(8,128)(2,1)} %get-tuple-element.82), channel_id=1, source_target_pairs={{0,1},{1,0},{2,3},{3,2},{4,5},{5,4},{6,7},{7,6},{8,9},{9,8},{10,11... | collective-permute-start | bytes 1769480 | tf_op jit(solution)/shard_map/ppermute | solution.py:832
  58.6 8.4 %collective-permute-start.7 = (bf16[576,256]{1,0:T(8,128)(2,1)S(1)}, bf16[576,256]{1,0:T(8,128)(2,1)S(1)}, u32[]{:S(2)}, u32[]{:S(2)}) collective-permute-start(bf16[576,256]{1,0:T(8,128)(2,1)S(1)} %constant_dynamic-slice_fusion.1), channel_id=1, source_target_pairs={{0,4},{1,9},{2,6},{3,11},{4,0},{5,13},{6,2},{7,15},{8,12},{9,1},{1... | collective-permute-start | bytes 884744 | tf_op jit(solution)/shard_map/ppermute | solution.py:832
  67.2 8.4 %collective-permute-start.8 = (bf16[288,256]{1,0:T(8,128)(2,1)S(1)}, bf16[288,256]{1,0:T(8,128)(2,1)S(1)}, u32[]{:S(2)}, u32[]{:S(2)}) collective-permute-start(bf16[288,256]{1,0:T(8,128)(2,1)S(1)} %constant_dynamic-slice_fusion), channel_id=1, source_target_pairs={{0,8},{1,5},{2,10},{3,7},{4,12},{5,1},{6,14},{7,3},{8,0},{9,13},{1... | collective-permute-start | bytes 442376 | tf_op jit(solution)/shard_map/ppermute | solution.py:832
  75.6 10.7 %collective-permute-start.17 = (bf16[288,256]{1,0:T(8,128)(2,1)S(1)}, bf16[288,256]{1,0:T(8,128)(2,1)S(1)}, u32[]{:S(2)}, u32[]{:S(2)}) collective-permute-start(bf16[288,256]{1,0:T(8,128)(2,1)S(1)} %dynamic-slice_add_fusion.1), channel_id=1, source_target_pairs={{0,16},{1,3},{2,18},{3,1},{4,20},{5,7},{6,22},{7,5},{8,24},{9,11},... | collective-permute-start | bytes 442376 | tf_op jit(solution)/shard_map/ppermute | solution.py:832
  86.3 2.7 %collective-permute-start.11 = (bf16[384,256]{1,0:T(8,128)(2,1)S(1)}, bf16[384,256]{1,0:T(8,128)(2,1)S(1)}, u32[]{:S(2)}, u32[]{:S(2)}) collective-permute-start(bf16[384,256]{1,0:T(8,128)(2,1)S(1)} %get-tuple-element.105), channel_id=1, source_target_pairs={{0,1},{1,0},{2,3},{3,2},{4,5},{5,4},{6,7},{7,6},{8,9},{9,8},{10,11... | collective-permute-start | bytes 589832 | tf_op jit(solution)/shard_map/ppermute | solution.py:832
  86.4 5.2 %collective-permute-start.18 = (bf16[288,256]{1,0:T(8,128)(2,1)S(1)}, bf16[288,256]{1,0:T(8,128)(2,1)S(1)}, u32[]{:S(2)}, u32[]{:S(2)}) collective-permute-start(bf16[288,256]{1,0:T(8,128)(2,1)S(1)} %add.68), channel_id=1, source_target_pairs={{0,2},{1,17},{2,0},{3,19},{4,6},{5,21},{6,4},{7,23},{8,10},{9,25},... | collective-permute-start | bytes 442376 | tf_op jit(solution)/shard_map/ppermute | solution.py:832
  89.1 6.0 %collective-permute-start.12 = (bf16[432,256]{1,0:T(8,128)(2,1)S(1)}, bf16[432,256]{1,0:T(8,128)(2,1)S(1)}, u32[]{:S(2)}, u32[]{:S(2)}) collective-permute-start(bf16[432,256]{1,0:T(8,128)(2,1)S(1)} %shard_map.196.a_ref), channel_id=1, source_target_pairs={{0,4},{1,9},{2,6},{3,11},{4,0},{5,13},{6,2},{7,15},{8,12},{9,1},{1... | collective-permute-start | bytes 663560 | tf_op jit(solution)/shard_map/ppermute | solution.py:832
  92.3 5.5 %collective-permute-start.19 = (bf16[288,256]{1,0:T(8,128)(2,1)}, bf16[288,256]{1,0:T(8,128)(2,1)}, u32[]{:S(2)}, u32[]{:S(2)}) collective-permute-start(bf16[288,256]{1,0:T(8,128)(2,1)} %add.69), channel_id=1, source_target_pairs={{0,8},{1,5},{2,10},{3,7},{4,12},{5,1},{6,14},{7,3},{8,0},{9,13},{1... | collective-permute-start | bytes 442376 | tf_op jit(solution)/shard_map/ppermute | solution.py:832
  92.8 9.7 %collective-permute-start.9 = (bf16[1024,256]{1,0:T(8,128)(2,1)}, bf16[1024,256]{1,0:T(8,128)(2,1)}, u32[]{:S(2)}, u32[]{:S(2)}) collective-permute-start(bf16[1024,256]{1,0:T(8,128)(2,1)} %get-tuple-element.99), channel_id=1, source_target_pairs={{0,1},{1,0},{2,3},{3,2},{4,5},{5,4},{6,7},{7,6},{8,9},{9,8},{10,11... | collective-permute-start | bytes 1572872 | tf_op jit(solution)/shard_map/ppermute | solution.py:832
  95.1 6.0 %collective-permute-start.13 = (bf16[432,256]{1,0:T(8,128)(2,1)S(1)}, bf16[432,256]{1,0:T(8,128)(2,1)S(1)}, u32[]{:S(2)}, u32[]{:S(2)}) collective-permute-start(bf16[432,256]{1,0:T(8,128)(2,1)S(1)} %shard_map.197.a_ref), channel_id=1, source_target_pairs={{0,8},{1,5},{2,10},{3,7},{4,12},{5,1},{6,14},{7,3},{8,0},{9,13},{1... | collective-permute-start | bytes 663560 | tf_op jit(solution)/shard_map/ppermute | solution.py:832
  99.7 7.0 %collective-permute-start.20 = (bf16[576,256]{1,0:T(8,128)(2,1)}, bf16[576,256]{1,0:T(8,128)(2,1)}, u32[]{:S(2)}, u32[]{:S(2)}) collective-permute-start(bf16[576,256]{1,0:T(8,128)(2,1)} %maximum_select_fusion.2), channel_id=1, source_target_pairs={{0,4},{1,9},{2,6},{3,11},{4,0},{5,13},{6,2},{7,15},{8,12},{9,1},{1... | collective-permute-start | bytes 884744 | tf_op jit(solution)/shard_map/ppermute | solution.py:832
  101.2 9.3 %collective-permute-start.14 = (bf16[432,256]{1,0:T(8,128)(2,1)S(1)}, bf16[432,256]{1,0:T(8,128)(2,1)S(1)}, u32[]{:S(2)}, u32[]{:S(2)}) collective-permute-start(bf16[432,256]{1,0:T(8,128)(2,1)S(1)} %shard_map.198.a_ref), channel_id=1, source_target_pairs={{0,16},{1,3},{2,18},{3,1},{4,20},{5,7},{6,22},{7,5},{8,24},{9,11},... | collective-permute-start | bytes 663560 | tf_op jit(solution)/shard_map/ppermute | solution.py:832
  105.0 14.8 %collective-permute-start.10 = (bf16[512,256]{1,0:T(8,128)(2,1)}, bf16[512,256]{1,0:T(8,128)(2,1)S(1)}, u32[]{:S(2)}, u32[]{:S(2)}) collective-permute-start(bf16[512,256]{1,0:T(8,128)(2,1)} %get-tuple-element.101), channel_id=1, source_target_pairs={{0,2},{1,3},{2,0},{3,1},{4,6},{5,7},{6,4},{7,5},{8,10},{9,11},{10,... | collective-permute-start | bytes 786440 | tf_op jit(solution)/shard_map/ppermute | solution.py:832
  110.5 9.1 %collective-permute-start.15 = (bf16[432,256]{1,0:T(8,128)(2,1)S(1)}, bf16[432,256]{1,0:T(8,128)(2,1)S(1)}, u32[]{:S(2)}, u32[]{:S(2)}) collective-permute-start(bf16[432,256]{1,0:T(8,128)(2,1)S(1)} %shard_map.199.a_ref), channel_id=1, source_target_pairs={{0,2},{1,17},{2,0},{3,19},{4,6},{5,21},{6,4},{7,23},{8,10},{9,25},... | collective-permute-start | bytes 663560 | tf_op jit(solution)/shard_map/ppermute | solution.py:832
  117.2 5.0 %collective-permute-start.21 = (bf16[1152,256]{1,0:T(8,128)(2,1)S(1)}, bf16[1152,256]{1,0:T(8,128)(2,1)S(1)}, u32[]{:S(2)}, u32[]{:S(2)}) collective-permute-start(bf16[1152,256]{1,0:T(8,128)(2,1)S(1)} %maximum_select_fusion.1.own_ref), channel_id=1, source_target_pairs={{0,1},{1,0},{2,3},{3,2},{4,5},{5,4},{6,7},{7,6},{8,9},{9,8},{10,11... | collective-permute-start | bytes 1769480 | tf_op jit(solution)/shard_map/ppermute | solution.py:832
  119.7 1.5 %collective-permute-start.16 = (bf16[432,256]{1,0:T(8,128)(2,1)S(1)}, bf16[432,256]{1,0:T(8,128)(2,1)S(1)}, u32[]{:S(2)}, u32[]{:S(2)}) collective-permute-start(bf16[432,256]{1,0:T(8,128)(2,1)S(1)} %shard_map.200.own_ref), channel_id=1, source_target_pairs={{0,1},{1,0},{2,3},{3,2},{4,5},{5,4},{6,7},{7,6},{8,9},{9,8},{10,11... | collective-permute-start | bytes 663560 | tf_op jit(solution)/shard_map/ppermute | solution.py:832
  (24 other events, 115.4 us)
